TPU v7x, 128 devices: a whole 4x4x4 slice. The times are simulated.
128 devices in a mesh: sess: 16 (over y, x), mp: 8 (over z, core).
Axes of the slice: x: 4, y: 4, z: 4, core: 2. Of those that a mesh axis runs over, the one named last changes fastest.
Arguments:
- mamba_x: bfloat16 [8192, 8192], P('sess', 'mp')
- gate_z: bfloat16 [8192, 8192], P('sess', 'mp'), may hold values from -6 to 6
- proj_bc: bfloat16 [8192, 2, 4, 256], P('sess'), may hold values from -6 to 6
- step_raw: float32 [128, 8192], P('mp', 'sess')
- step_bias: float32 [128], P('mp'), may hold values from -4.5 to -3.5
- decay_log: float32 [128], P('mp')
- skip_gain: float32 [128], P('mp'), may hold values from 0.5 to 1.5
- norm_gain: float32 [8192], P('mp'), may hold values from 0.1 to 1.9
- state_cache: bfloat16 [256, 128, 64, 256], P('sess', 'mp'), may hold values from -1.1953125 to 1.1953125
- cache_slot: int32 [256], replicated, may hold values from 0 to 255, as said below
- prefix_pages: int32 [256], P('sess'), may hold values from 1 to 4
- page_table: int32 [256, 4], replicated, may hold values from 0 to 63, as said below
- queries: bfloat16 [8192, 8192], P('sess', 'mp')
- appended_memory_pair: bfloat16 [8192, 2, 8, 128], P('sess', None, 'mp')
- key_value_pages: bfloat16 [1024, 64, 2, 8, 128], P('sess', None, None, 'mp'), may hold values from -6 to 6
Outputs:
- mamba_out: bfloat16 [8192, 8192], P('sess', 'mp')
- new_state: bfloat16 [256, 128, 64, 256], P('sess', 'mp')
- attn_out: bfloat16 [8192, 8192], P('sess', 'mp')
Inputs may be any that keep to these rules, and one draw needn't show every extreme that they name: cache_slot is a permutation of the 256 slots; slot c is held by the owner c // 16 on sess at local slot c % 16; among the 16 sessions of one index of sess at most 2 have their caches on one owner, and that many do in every draw. `page_table`: entries are page indices in the pool of the session's owner; the 4 entries of a session are distinct and no page serves two sessions.
All inputs are finite; a program needn't handle non-finite values.
Results may differ from a plain program's by a relative error of at most 0.0049.
Values may be sent and summed in bfloat16 or wider, within the bound.
No kernel may reach another device: no remote copies, remote signals or barrier semaphores. Data moves between devices by JAX's collectives and lax.ppermute only.
A program may use at most 192 MiB of HBM per device.

v0:
```python
import jax
import jax.numpy as jnp
from jax import lax
from jax.sharding import PartitionSpec as P

HM = 128
P_SIZE = 64
NS = 256
G = 4
HEAD_WIDTH = 128
CAP = 2
PAGE_TOKENS = 64


EPS = 1e-05


def swapped(block, axis, stride):
    count = lax.axis_size(axis)
    route = []
    for low in range(count):
        high = low | 1 << stride
        if high != low and high < count:
            route += [(low, high), (high, low)]
    return lax.ppermute(block, axis, route)


def send_plan(cache_slot, page_table, sender, slots):
    blocks = cache_slot.shape[0] // slots
    owner_grid = (cache_slot // slots).reshape(blocks, slots)
    local_grid = (cache_slot % slots).reshape(blocks, slots)
    mine = (owner_grid == sender).astype(jnp.int32)
    before = jnp.cumsum(mine, axis=1) - mine
    which = jnp.arange(CAP, dtype=jnp.int32)
    match = mine[:, None, :] * (before[:, None, :] == which[None, :, None]).astype(jnp.int32)
    send_slots = jnp.sum(match * local_grid[:, None, :], axis=2)
    tables = page_table.reshape(blocks, 1, slots, page_table.shape[1])
    send_pages = jnp.sum(match[:, :, :, None] * tables, axis=2)
    return (send_slots, send_pages)


def pick_plan(cache_slot, receiver, slots):
    own_row = lax.dynamic_slice_in_dim(cache_slot, receiver * slots, slots) // slots
    same_owner = (own_row[:, None] == own_row[None, :]).astype(jnp.int32)
    position = jnp.arange(slots)
    earlier = (position[None, :] < position[:, None]).astype(jnp.int32)
    ranked = jnp.sum(same_owner * earlier, axis=1)
    return own_row * CAP + ranked


def group_total(squares):
    total = squares
    total = total + swapped(total, "mp", 0)
    return total


def mamba_part(
    mamba_x, gate_z, proj_bc, step_raw, step_bias, decay_log, skip_gain, norm_gain, start_state
):
    slots = start_state.shape[0]
    heads = step_raw.shape[0]
    prefix_length = mamba_x.shape[0] // slots
    group = lax.axis_index("mp") * heads // (HM // G)
    both = lax.dynamic_index_in_dim(proj_bc, group, axis=2, keepdims=False)
    inputs_b = both[:, 0].reshape(slots, prefix_length, NS)
    inputs_c = both[:, 1].reshape(slots, prefix_length, NS)
    delta = jax.nn.softplus(step_raw + step_bias[:, None]).reshape(heads, slots, prefix_length)
    falloff_factor = -jnp.exp(decay_log)[:, None, None] * delta
    position = jnp.arange(prefix_length)
    lower = (position[:, None] >= position[None, :]).astype(jnp.float32)
    cumul = jnp.einsum("hsu,tu->hst", falloff_factor, lower, precision=lax.Precision.HIGHEST)
    causal = lower > 0
    spread = cumul[:, :, :, None] - cumul[:, :, None, :]
    decay = jnp.where(causal, jnp.exp(jnp.where(causal, spread, 0.0)), 0.0)
    inner = jnp.einsum("stn,sun->stu", inputs_c, inputs_b, preferred_element_type=jnp.float32)
    weights = (inner[None] * decay * delta[:, :, None, :]).astype(jnp.bfloat16)
    values = mamba_x.reshape(slots, prefix_length, heads, P_SIZE)
    intra = jnp.einsum("hstu,suhp->sthp", weights, values, preferred_element_type=jnp.float32)
    carried = jnp.einsum(
        "stn,shpn->sthp", inputs_c, start_state, preferred_element_type=jnp.float32
    )
    expansion_factor = jnp.exp(cumul).transpose(1, 2, 0)[:, :, :, None]
    output = (
        intra
        + carried * expansion_factor
        + skip_gain[None, None, :, None] * values.astype(jnp.float32)
    )
    gates = gate_z.reshape(slots, prefix_length, heads, P_SIZE).astype(jnp.float32)
    gated = output * jax.nn.silu(gates)
    squares = jnp.sum(gated * gated, axis=(2, 3)).reshape(slots * prefix_length)
    total = group_total(squares)
    scale = lax.rsqrt(total / (HM // G * P_SIZE) + EPS)
    normed = (
        gated.reshape(slots * prefix_length, heads * P_SIZE) * scale[:, None] * norm_gain[None, :]
    )
    last_cumul = cumul[:, :, prefix_length - 1 :]
    tail = jnp.exp(last_cumul - cumul) * delta
    scaled = (values.astype(jnp.float32) * tail.transpose(1, 2, 0)[:, :, :, None]).astype(
        jnp.bfloat16
    )
    local = jnp.einsum("suhp,sun->shpn", scaled, inputs_b, preferred_element_type=jnp.float32)
    carry_decay = jnp.exp(last_cumul[:, :, 0]).T[:, :, None, None]
    fresh = carry_decay * start_state.astype(jnp.float32) + local
    return (normed.astype(jnp.bfloat16), fresh.astype(jnp.bfloat16))


def attend(queries, appended_memory_pair, prefix_kv, prefix_pages):
    slots = prefix_pages.shape[0]
    prefix_length = queries.shape[0] // slots
    kv_heads = appended_memory_pair.shape[2]
    grouped = queries.shape[1] // (kv_heads * HEAD_WIDTH)
    fresh_kv = appended_memory_pair.reshape(slots, prefix_length, 2, kv_heads, HEAD_WIDTH)
    keyvals = jnp.concatenate([prefix_kv, fresh_kv], axis=1)
    kept = prefix_kv.shape[1]
    requested = queries.reshape(slots, prefix_length, kv_heads, grouped, HEAD_WIDTH)
    scores = jnp.einsum(
        "stkgd,sjkd->skgtj", requested, keyvals[:, :, 0], preferred_element_type=jnp.float32
    ) * HEAD_WIDTH ** (-0.5)
    column = jnp.arange(kept + prefix_length)
    row_pos = jnp.arange(prefix_length)
    limit = prefix_pages * PAGE_TOKENS
    valid_prefix = column[None, :] < limit[:, None]
    valid_new = column[None, :] - kept <= row_pos[:, None]
    valid = jnp.where(column[None, None, :] < kept, valid_prefix[:, None, :], valid_new[None, :, :])
    scores = jnp.where(valid[:, None, None], scores, -jnp.inf)
    peak = jnp.max(scores, axis=-1, keepdims=True)
    expo = jnp.exp(scores - peak)
    probs = (expo / jnp.sum(expo, axis=-1, keepdims=True)).astype(jnp.bfloat16)
    mixed = jnp.einsum(
        "skgtj,sjkd->stkgd", probs, keyvals[:, :, 1], preferred_element_type=jnp.float32
    )
    return mixed.reshape(slots * prefix_length, kv_heads * grouped * HEAD_WIDTH).astype(
        jnp.bfloat16
    )


def shards(
    mamba_x,
    gate_z,
    proj_bc,
    step_raw,
    step_bias,
    decay_log,
    skip_gain,
    norm_gain,
    state_cache,
    cache_slot,
    prefix_pages,
    page_table,
    queries,
    appended_memory_pair,
    key_value_pages,
):
    slots = state_cache.shape[0]
    device_here = lax.axis_index("sess")
    send_slots, send_pages = send_plan(cache_slot, page_table, device_here, slots)
    picked = pick_plan(cache_slot, device_here, slots)
    state_send = jnp.take(state_cache, send_slots.reshape(-1), axis=0).reshape(
        send_slots.shape + state_cache.shape[1:]
    )
    page_send = jnp.take(key_value_pages, send_pages.reshape(-1), axis=0).reshape(
        send_slots.shape
        + (send_pages.shape[2] * key_value_pages.shape[1],)
        + key_value_pages.shape[2:]
    )
    got_states, got_pages = (
        lax.all_to_all(state_send, "sess", split_axis=0, concat_axis=0, tiled=True),
        lax.all_to_all(page_send, "sess", split_axis=0, concat_axis=0, tiled=True),
    )
    start_state = jnp.take(got_states.reshape((-1,) + state_cache.shape[1:]), picked, axis=0)
    mixed, fresh = mamba_part(
        mamba_x, gate_z, proj_bc, step_raw, step_bias, decay_log, skip_gain, norm_gain, start_state
    )
    prefix_kv = jnp.take(got_pages.reshape((-1,) + page_send.shape[2:]), picked, axis=0)
    attended = attend(queries, appended_memory_pair, prefix_kv, prefix_pages)
    return (mixed, fresh, attended)


def solution(mesh):
    return jax.shard_map(
        shards,
        mesh=mesh,
        in_specs=(
            P("sess", "mp"),
            P("sess", "mp"),
            P("sess", None, None, None),
            P("mp", "sess"),
            P("mp"),
            P("mp"),
            P("mp"),
            P("mp"),
            P("sess", "mp", None, None),
            P(),
            P("sess"),
            P(),
            P("sess", "mp"),
            P("sess", None, "mp", None),
            P("sess", None, None, "mp", None),
        ),
        out_specs=(P("sess", "mp"), P("sess", "mp", None, None), P("sess", "mp")),
        check_vma=False,
    )
```

profile of v0, /device:TPU:1, one launch (start us, length us, event | category | flops | bytes accessed | tf_op | source)
XLA Modules:
  0.0 394.0 jit_solution(15228423363149924306)
XLA Ops:
  3.9 3.5 copy.156
  7.4 4.7 %gather_fusion.2 = bf16[128,64,2,128]{3,1,2,0:T(8,128)(2,1)} fusion(bf16[64,64,2,128]{3,1,2,0:T(8,128)(2,1)} %bitcast.104, s32[1024]{0:T(1024)S(1)} %pad_clamp_fusion), kind=kCustom, calls=%fused_computation.2 | custom fusion | bytes 8389120 | tf_op jit(solution)/shard_map/jit(_take)/gather | solution.py:161
  12.1 5.3 %copy.126 = bf16[128,64,2,128]{3,1,0,2:T(8,128)(2,1)} copy(bf16[128,64,2,128]{3,1,2,0:T(8,128)(2,1)} %gather_fusion.2) | data formatting | bytes 8388608 | tf_op jit(solution)/shard_map/jit(_take)/gather | solution.py:161
  17.7 3.6 broadcast_select_fusion.2
  21.4 2.3 copy.127
  23.6 7.6 %all-to-all-start.1 = ((bf16[16,2,256,2,1,128]{5,2,3,1,4,0:T(8,128)(2,1)}), bf16[16,2,256,2,1,128]{5,2,3,1,4,0:T(8,128)(2,1)}, u32[]{:S(2)}, u32[]{:S(2)}) async-start(bf16[16,2,256,2,1,128]{5,2,3,1,4,0:T(8,128)(2,1)} %copy.127), calls=%async_computation.1 | async-start | bytes 8388608 | tf_op jit(solution)/shard_map/all_to_all | solution.py:168
  31.6 10.6 %gather_fusion = bf16[32,16,64,256]{3,2,1,0:T(8,128)(2,1)} fusion(bf16[16,16,64,256]{3,2,1,0:T(8,128)(2,1)} %param.23, s32[1024]{0:T(1024)S(1)} %pad_clamp_fusion.2), kind=kCustom, calls=%fused_computation | custom fusion | bytes 33554560 | tf_op jit(solution)/shard_map/jit(_take)/gather | solution.py:158
  42.2 14.1 %broadcast_select_fusion = bf16[16,2,16,64,256]{4,3,2,1,0:T(8,128)(2,1)} fusion(bf16[16,2,16,64,256]{4,3,2,1,0:T(8,128)(2,1)} %bitcast.103, pred[16,2]{1,0:T(8,128)(4,1)S(1)} %copy.113), kind=kLoop, calls=%fused_computation.5 | loop fusion | flops 8388608 | bytes 33554464 | tf_op jit(solution)/shard_map/jit(_take)/select_n | solution.py:158
  56.3 37.3 %all-to-all-done.1 = bf16[16,2,256,2,1,128]{5,2,3,1,4,0:T(8,128)(2,1)} async-done(((bf16[16,2,256,2,1,128]{5,2,3,1,4,0:T(8,128)(2,1)}), bf16[16,2,256,2,1,128]{5,2,3,1,4,0:T(8,128)(2,1)}, u32[]{:S(2)}, u32[]{:S(2)}) %all-to-all-start.1) | async-done | bytes 4194336 | tf_op jit(solution)/shard_map/all_to_all | solution.py:168
  93.6 5.3 %all-to-all-start = ((bf16[16,2,16,64,256]{4,3,2,1,0:T(8,128)(2,1)}), bf16[16,2,16,64,256]{4,3,2,1,0:T(8,128)(2,1)}, u32[]{:S(2)}, u32[]{:S(2)}) async-start(bf16[16,2,16,64,256]{4,3,2,1,0:T(8,128)(2,1)} %broadcast_select_fusion), calls=%async_computation | async-start | bytes 33554432 | tf_op jit(solution)/shard_map/all_to_all | solution.py:167
  104.8 2.4 reshape.268
  107.1 4.1 %reshape.281 = f32[16,32,16,64]{3,2,1,0:T(8,128)} reshape(bf16[512,1024]{1,0:T(8,128)(2,1)} %param.16) | data formatting | bytes 3145728 | tf_op jit(solution)/shard_map/convert_element_type | solution.py:88
  113.6 4.3 %gather_fusion.3 = bf16[16,256,2,128]{3,1,2,0:T(8,128)(2,1)} fusion(bf16[32,256,2,128]{3,1,2,0:T(8,128)(2,1)} %bitcast.18, s32[1024]{0:T(1024)S(1)} %pad_clamp_fusion.1), kind=kCustom, calls=%fused_computation.3 | custom fusion | bytes 4194368 | tf_op jit(solution)/shard_map/jit(_take)/gather | solution.py:174
  121.0 2.1 fusion
  123.2 2.2 fusion.22
  127.1 215.8 %all-to-all-done = bf16[16,2,16,64,256]{4,3,2,1,0:T(8,128)(2,1)} async-done(((bf16[16,2,16,64,256]{4,3,2,1,0:T(8,128)(2,1)}), bf16[16,2,16,64,256]{4,3,2,1,0:T(8,128)(2,1)}, u32[]{:S(2)}, u32[]{:S(2)}) %all-to-all-start) | async-done | bytes 16777248 | tf_op jit(solution)/shard_map/all_to_all | solution.py:167
  342.9 10.7 %gather_fusion.1 = bf16[16,16,64,256]{3,2,1,0:T(8,128)(2,1)} fusion(bf16[32,16,64,256]{3,2,1,0:T(8,128)(2,1)} %bitcast.9, s32[1024]{0:T(1024)S(1)} %pad_clamp_fusion.1), kind=kCustom, calls=%fused_computation.1 | custom fusion | bytes 16777280 | tf_op jit(solution)/shard_map/jit(_take)/gather | solution.py:170
  353.6 7.6 %fusion.5 = f32[16,32,16,64]{3,1,2,0:T(8,128)S(1)} fusion(bf16[16,32,256,1]{2,1,3,0:T(8,128)(2,1)S(1)} %bitcast.116, bf16[16,16,64,256]{3,2,1,0:T(8,128)(2,1)} %gather_fusion.1, pred[16]{0:T(512)(128)(4,1)S(1)} %get-tuple-element.3), kind=kOutput, calls=%fused_computation.21 | convolution fusion | flops 272629760 | bytes 10747920 | tf_op jit(solution)/shard_map/stn,shpn->sthp/dot_general | solution.py:79
  361.4 7.7 %multiply_reduce_fusion = (f32[16,32]{1,0:T(8,128)S(1)}, f32[16,32,16,64]{3,1,2,0:T(8,128)}) fusion(f32[16,32,16,64]{3,2,1,0:T(8,128)S(1)} %copy-done.2, bf16[16,32,16,64]{3,2,1,0:T(8,128)(2,1)S(1)} %copy-done.4, f32[16]{0:T(128)S(1)} %copy-done.22, f32[16,32,16,64]{3,1,2,0:T(8,128)S(1)} %fusion.5, f32[16,32,16]{1,2,0:T(8,128)S(1)} %copy-done.15, ...), kind=kOutput, calls=%fused_computation.18 | convolution fusion | flops 41418240 | bytes 7507008 | tf_op jit(solution)/shard_map/hstu,suhp->sthp/dot_general | solution.py:78
  369.2 2.7 collective-permute-start
  371.9 9.2 %add_convert_fusion = bf16[16,16,64,256]{3,2,1,0:T(8,128)(2,1)} fusion(bf16[16,32,256,1]{2,1,3,0:T(8,128)(2,1)S(1)} %bitcast.114, f32[16,16]{1,0:T(8,128)S(1)} %copy.120, bf16[16,16,64,256]{3,2,1,0:T(8,128)(2,1)} %gather_fusion.1, pred[16]{0:T(512)(128)(4,1)S(1)} %get-tuple-element.3, f32[16,32,16]{1,2,0:T(8,128)S(1)} %copy-done.13, ...), kind=kOutput, calls=%fused_computation.4 | convolution fusion | flops 290979840 | bytes 18121744 | tf_op jit(solution)/shard_map/suhp,sun->shpn/dot_general | solution.py:101
  381.1 5.2 %copy.119 = f32[16,32,16,64]{3,2,1,0:T(8,128)} copy(f32[16,32,16,64]{3,1,2,0:T(8,128)S(1)} %copy-done.3) | data formatting | bytes 4194304 | tf_op jit(solution)/shard_map/mul | solution.py:89
  386.3 4.9 %reshape.271 = f32[512,1024]{1,0:T(8,128)} reshape(f32[16,32,16,64]{3,2,1,0:T(8,128)} %copy.119) | data formatting | bytes 4194304 | tf_op jit(solution)/shard_map/reshape | solution.py:94
  391.2 2.8 multiply_convert_fusion.2
  (106 shorter events, 16.7 us)
Async XLA Ops:
  0.6 100.7 %copy-start = (bf16[512,2,4,256]{3,2,1,0:T(4,128)(2,1)S(1)}, bf16[512,2,4,256]{3,2,1,0:T(4,128)(2,1)}, u32[]{:S(2)}) copy-start(bf16[512,2,4,256]{3,2,1,0:T(4,128)(2,1)} %param.17) | copy-start | bytes 6291460
  23.6 70.0 %all-to-all-start.1 = ((bf16[16,2,256,2,1,128]{5,2,3,1,4,0:T(8,128)(2,1)}), bf16[16,2,256,2,1,128]{5,2,3,1,4,0:T(8,128)(2,1)}, u32[]{:S(2)}, u32[]{:S(2)}) async-start(bf16[16,2,256,2,1,128]{5,2,3,1,4,0:T(8,128)(2,1)} %copy.127), calls=%async_computation.1 | async-start | bytes 8388608 | tf_op jit(solution)/shard_map/all_to_all | solution.py:168
  56.3 42.7 %copy-start.12 = (bf16[512,2,1,128]{3,1,2,0:T(2,128)(2,1)S(1)}, bf16[512,2,1,128]{3,1,2,0:T(2,128)(2,1)}, u32[]{:S(2)}) copy-start(bf16[512,2,1,128]{3,1,2,0:T(2,128)(2,1)} %param.28) | copy-start | bytes 786436
  93.6 249.2 %all-to-all-start = ((bf16[16,2,16,64,256]{4,3,2,1,0:T(8,128)(2,1)}), bf16[16,2,16,64,256]{4,3,2,1,0:T(8,128)(2,1)}, u32[]{:S(2)}, u32[]{:S(2)}) async-start(bf16[16,2,16,64,256]{4,3,2,1,0:T(8,128)(2,1)} %broadcast_select_fusion), calls=%async_computation | async-start | bytes 33554432 | tf_op jit(solution)/shard_map/all_to_all | solution.py:167
  99.0 3.5 copy-start.16
  99.0 3.5 copy-start.19
  99.0 3.8 copy-start.20
  104.8 7.3 %copy-start.17 = (s32[256]{0:T(256)S(1)}, s32[256]{0:T(256)}, u32[]{:S(2)}) copy-start(s32[256]{0:T(256)} %param.24) | copy-start | bytes 3076
  104.8 7.7 %copy-start.21 = (s32[16]{0:T(128)S(1)}, s32[16]{0:T(128)}, u32[]{:S(2)}) copy-start(s32[16]{0:T(128)} %param.25) | copy-start | bytes 196
  112.7 5.2 %copy-start.7 = (bf16[512,1,256]{2,0,1:T(8,128)(2,1)}, bf16[512,1,256]{2,0,1:T(8,128)(2,1)S(1)}, u32[]{:S(2)}) copy-start(bf16[512,1,256]{2,0,1:T(8,128)(2,1)S(1)} %get-tuple-element.5) | copy-start | bytes 786436
  112.7 5.2 %copy-start.9 = (bf16[512,1,256]{2,0,1:T(8,128)(2,1)}, bf16[512,1,256]{2,0,1:T(8,128)(2,1)S(1)}, u32[]{:S(2)}) copy-start(bf16[512,1,256]{2,0,1:T(8,128)(2,1)S(1)} %get-tuple-element.6) | copy-start | bytes 786436
  342.9 10.8 %copy-start.10 = (bf16[512,1,256]{2,0,1:T(8,128)(2,1)S(1)}, bf16[512,1,256]{2,0,1:T(8,128)(2,1)}, u32[]{:S(2)}) copy-start(bf16[512,1,256]{2,0,1:T(8,128)(2,1)} %copy-done.9) | copy-start | bytes 786436
  353.6 7.7 %copy-start.2 = (f32[16,32,16,64]{3,2,1,0:T(8,128)S(1)}, f32[16,32,16,64]{3,2,1,0:T(8,128)}, u32[]{:S(2)}) copy-start(f32[16,32,16,64]{3,2,1,0:T(8,128)} %reshape.281) | copy-start | bytes 6291460
  353.6 7.7 %copy-start.4 = (bf16[16,32,16,64]{3,2,1,0:T(8,128)(2,1)S(1)}, bf16[16,32,16,64]{3,2,1,0:T(8,128)(2,1)}, u32[]{:S(2)}) copy-start(bf16[16,32,16,64]{3,2,1,0:T(8,128)(2,1)} %reshape.268) | copy-start | bytes 3145732
  353.6 7.7 %copy-start.11 = (f32[16,32,32]{2,1,0:T(8,128)S(1)}, f32[16,32,32]{2,1,0:T(8,128)}, u32[]{:S(2)}) copy-start(f32[16,32,32]{2,1,0:T(8,128)} %fusion.48) | copy-start | bytes 196612
  353.6 7.7 %copy-start.14 = (f32[16,16,32]{2,0,1:T(8,128)S(1)}, f32[16,16,32]{2,0,1:T(8,128)}, u32[]{:S(2)}) copy-start(f32[16,16,32]{2,0,1:T(8,128)} %copy.109) | copy-start | bytes 98308
  353.6 7.7 %copy-start.15 = (f32[16,32,16]{1,2,0:T(8,128)S(1)}, f32[16,32,16]{1,2,0:T(8,128)}, u32[]{:S(2)}) copy-start(f32[16,32,16]{1,2,0:T(8,128)} %copy.115) | copy-start | bytes 98308
  353.6 7.7 %copy-start.22 = (f32[16]{0:T(128)S(1)}, f32[16]{0:T(128)}, u32[]{:S(2)}) copy-start(f32[16]{0:T(128)} %param.21) | copy-start | bytes 196
  361.4 10.6 %copy-start.8 = (bf16[512,1,256]{2,0,1:T(8,128)(2,1)S(1)}, bf16[512,1,256]{2,0,1:T(8,128)(2,1)}, u32[]{:S(2)}) copy-start(bf16[512,1,256]{2,0,1:T(8,128)(2,1)} %copy-done.7) | copy-start | bytes 786436
  361.4 10.5 %copy-start.13 = (f32[16,32,16]{1,2,0:T(8,128)S(1)}, f32[16,32,16]{1,2,0:T(8,128)}, u32[]{:S(2)}) copy-start(f32[16,32,16]{1,2,0:T(8,128)} %copy.121) | copy-start | bytes 98308
  369.2 22.0 %collective-permute-start = (f32[512]{0:T(512)S(1)}, f32[512]{0:T(512)S(1)}, u32[]{:S(2)}, u32[]{:S(2)}) collective-permute-start(f32[512]{0:T(512)S(1)} %reshape.272), channel_id=1, source_target_pairs={{0,1},{1,0},{2,3},{3,2},{4,5},{5,4},{6,7},{7,6},{8,9},{9,8},{10,11... | collective-permute-start | bytes 6152 | tf_op jit(solution)/shard_map/ppermute | solution.py:25
  371.9 9.2 %copy-start.3 = (f32[16,32,16,64]{3,1,2,0:T(8,128)S(1)}, f32[16,32,16,64]{3,1,2,0:T(8,128)}, u32[]{:S(2)}) copy-start(f32[16,32,16,64]{3,1,2,0:T(8,128)} %get-tuple-element.12) | copy-start | bytes 6291460
  381.1 12.9 %copy-start.1 = (bf16[512,2,4,256]{3,2,1,0:T(4,128)(2,1)S(1)}, bf16[512,2,4,256]{3,2,1,0:T(4,128)(2,1)}, u32[]{:S(2)}) copy-start(bf16[512,2,4,256]{3,2,1,0:T(4,128)(2,1)} %param.17) | copy-start | bytes 6291460
  386.3 4.9 %copy-start.18 = (f32[1024]{0:T(1024)S(1)}, f32[1024]{0:T(1024)}, u32[]{:S(2)}) copy-start(f32[1024]{0:T(1024)} %param.22) | copy-start | bytes 12292
  (2 other events, 4.3 us)
where the time goes:
time: 395 us; the launch traced here: 394 us
  waiting for transfers between devices  253 us (64%)
  local copies, waits for them, and re-layouts  67.6 us (17%)
  matrix products  29.1 us (7%)
  other arithmetic  27.4 us (7%)
  starting transfers between devices  15.7 us (4%)
    all_to_all x1, waiting for transfers between devices, shards(): lax.all_to_all(state_send, 'sess', split_axis=0, concat_axis=0, tiled=True)  216 us
    all_to_all x1, waiting for transfers between devices, shards(): lax.all_to_all(page_send, 'sess', split_axis=0, concat_axis=0, tiled=True)  37.3 us
    select_n x2, other arithmetic, shards(): jnp.take(state_cache, send_slots.reshape(-1), axis=0)  14.2 us
    gather x1, local copies, waits for them, and re-layouts, shards(): jnp.take(got_states.reshape((-1,) + state_cache.shape[1:]), picked, axis=0)  10.7 us
    gather x1, local copies, waits for them, and re-layouts, shards(): jnp.take(state_cache, send_slots.reshape(-1), axis=0)  10.6 us
    gather x2, local copies, waits for them, and re-layouts, shards(): jnp.take(key_value_pages, send_pages.reshape(-1), axis=0)  10 us
    dot_general x1, matrix products, mamba_part(): jnp.einsum('suhp,sun->shpn', scaled, inputs_b, preferred_element_type=jnp...  9.2 us
  transfers between devices with their start and end apart: 3, of which 2 were waited for; matrix products, arithmetic and copies ran while one was open for 18% of the time, Pallas kernels for 0%

commit v1 on v0

--- a/solution.py
+++ b/solution.py
@@ -1,6 +1,10 @@
+import functools
+
 import jax
 import jax.numpy as jnp
 from jax import lax
+from jax.experimental import pallas as pl
+from jax.experimental.pallas import tpu as pltpu
 from jax.sharding import PartitionSpec as P
 
 HM = 128
@@ -10,9 +14,22 @@
 HEAD_WIDTH = 128
 CAP = 2
 PAGE_TOKENS = 64
-
-
 EPS = 1e-05
+
+STEPS = (10, 11, 12, 13, 14)
+DELAY = 1
+SIDE = 4
+HIGHEST = lax.Precision.HIGHEST
+F32 = jnp.float32
+BF16 = jnp.bfloat16
+
+
+def params():
+    return pltpu.CompilerParams(vmem_limit_bytes=56 * 1024 * 1024)
+
+
+def cost(flops, moved):
+    return pl.CostEstimate(flops=flops, bytes_accessed=moved, transcendentals=0)
 
 
 def swapped(block, axis, stride):
@@ -134,7 +151,7 @@
     )
 
 
-def shards(
+def padded(
     mamba_x,
     gate_z,
     proj_bc,
@@ -174,6 +191,439 @@
     prefix_kv = jnp.take(got_pages.reshape((-1,) + page_send.shape[2:]), picked, axis=0)
     attended = attend(queries, appended_memory_pair, prefix_kv, prefix_pages)
     return (mixed, fresh, attended)
+
+
+def dot(a, b, dims, precision=None):
+    return lax.dot_general(
+        a, b, ((dims[:1], dims[1:]), ((), ())), precision=precision, preferred_element_type=F32
+    )
+
+
+def spread_matrix(heads, lanes):
+    row = lax.broadcasted_iota(jnp.int32, (heads, heads * lanes), 0)
+    column = lax.broadcasted_iota(jnp.int32, (heads, heads * lanes), 1)
+    return (row == column // lanes).astype(F32)
+
+
+def spread(columns, lanes):
+    return dot(columns, spread_matrix(columns.shape[1], lanes), (1, 0), HIGHEST)
+
+
+def before_kernel(x_ref, b_ref, c_ref, cumul_ref, tail_ref, row_ref, skip_ref, base, scaled):
+    heads = cumul_ref.shape[2]
+    tokens = x_ref.shape[0]
+    quad = 4
+    x = x_ref[...]
+    inner = dot(c_ref[...], b_ref[...], (1, 1))
+    at_t = spread(cumul_ref[0], tokens)
+    row = lax.broadcasted_iota(jnp.int32, at_t.shape, 0)
+    column = lax.broadcasted_iota(jnp.int32, at_t.shape, 1)
+    causal = row >= column % tokens
+    gap = at_t - row_ref[0, 0:1]
+    decay = jnp.where(causal, jnp.exp(jnp.where(causal, gap, 0.0)), 0.0)
+    inner = jnp.concatenate([inner] * heads, axis=1)
+    weights = (inner * decay * row_ref[0, 1:2]).astype(BF16)
+    own_row = lax.broadcasted_iota(jnp.int32, (quad * tokens, quad * P_SIZE), 0) // tokens
+    own_column = lax.broadcasted_iota(jnp.int32, (quad * tokens, quad * P_SIZE), 1) // P_SIZE
+    own = own_row == own_column
+    for q in range(heads // quad):
+        lanes = slice(q * quad * P_SIZE, (q + 1) * quad * P_SIZE)
+        values = x[:, lanes].astype(F32)
+        stacked = jnp.where(own, jnp.concatenate([values] * quad, axis=0), 0.0).astype(BF16)
+        part = weights[:, q * quad * tokens : (q + 1) * quad * tokens]
+        base[:, lanes] = dot(part, stacked, (1, 0)) + skip_ref[:, lanes] * values
+    scaled[...] = (x.astype(F32) * spread(tail_ref[0], P_SIZE)).astype(BF16)
+
+
+def mamba_before(x, b, c, cumul, tail, rows, skip):
+    total, width = x.shape
+    slots, tokens, heads = cumul.shape
+    per = lambda shape: pl.BlockSpec(shape, lambda s: (s,) + (0,) * (len(shape) - 1))
+    return pl.pallas_call(
+        before_kernel,
+        grid=(slots,),
+        in_specs=[
+            per((tokens, width)),
+            per((tokens, NS)),
+            per((tokens, NS)),
+            per((1, tokens, heads)),
+            per((1, tokens, heads)),
+            per((1, 2, heads * tokens)),
+            pl.BlockSpec((1, width), lambda s: (0, 0)),
+        ],
+        out_specs=[per((tokens, width)), per((tokens, width))],
+        out_shape=[
+            jax.ShapeDtypeStruct((total, width), F32),
+            jax.ShapeDtypeStruct((total, width), BF16),
+        ],
+        compiler_params=params(),
+        cost_estimate=cost(10**9, 20 * 2**20),
+        name="mamba_before",
+    )(x, b, c, cumul, tail, rows, skip)
+
+
+def mamba_step(state, base, c, b, scaled, cumul, gate, carry, gated, squares, fresh):
+    heads = state.shape[0]
+    carried = dot(c, state.reshape(heads * P_SIZE, NS), (1, 1))
+    out = base + carried * spread(jnp.exp(cumul), P_SIZE)
+    gate = gate.astype(F32)
+    value = out * (gate / (1.0 + jnp.exp(-gate)))
+    gated[...] = value
+    ones = jnp.ones((8, value.shape[1]), F32)
+    squares[0] = dot(ones, value * value, (1, 1), HIGHEST)[0:1]
+    local = dot(scaled, b, (0, 0))
+    for h in range(heads):
+        rows = slice(h * P_SIZE, (h + 1) * P_SIZE)
+        fresh[0, h] = (carry[h : h + 1] * state[h].astype(F32) + local[rows]).astype(BF16)
+
+
+def attend_step(pages, queries, new, prefix, out):
+    kept = pages.shape[0]
+    tokens = queries.shape[0]
+    heads = queries.shape[1] // HEAD_WIDTH
+    q = jnp.concatenate(
+        [queries[:, g * HEAD_WIDTH : (g + 1) * HEAD_WIDTH] for g in range(heads)], axis=0
+    )
+    factor = HEAD_WIDTH ** (-0.5)
+    old_scores = dot(q, pages[:, :HEAD_WIDTH], (1, 1)) * factor
+    new_scores = dot(q, new[:, :HEAD_WIDTH], (1, 1)) * factor
+    column = lax.broadcasted_iota(jnp.int32, old_scores.shape, 1)
+    old_scores = jnp.where(column < prefix * PAGE_TOKENS, old_scores, -jnp.inf)
+    row = lax.broadcasted_iota(jnp.int32, new_scores.shape, 0) % tokens
+    column = lax.broadcasted_iota(jnp.int32, new_scores.shape, 1)
+    new_scores = jnp.where(column <= row, new_scores, -jnp.inf)
+    peak = jnp.maximum(
+        jnp.max(old_scores, axis=1, keepdims=True), jnp.max(new_scores, axis=1, keepdims=True)
+    )
+    old_expo = jnp.exp(old_scores - peak)
+    new_expo = jnp.exp(new_scores - peak)
+    total = jnp.sum(old_expo, axis=1, keepdims=True) + jnp.sum(new_expo, axis=1, keepdims=True)
+    old_probs = (old_expo / total).astype(BF16)
+    new_probs = (new_expo / total).astype(BF16)
+    mixed = dot(old_probs, pages[:, HEAD_WIDTH:], (1, 0)) + dot(
+        new_probs, new[:, HEAD_WIDTH:], (1, 0)
+    )
+    for g in range(heads):
+        out[:, g * HEAD_WIDTH : (g + 1) * HEAD_WIDTH] = mixed[
+            g * tokens : (g + 1) * tokens
+        ].astype(BF16)
+
+
+def schedule_kernel(most, dest_ref, table_ref, final_ref):
+    dest = dest_ref[...]
+    items = dest.shape[1]
+    nodes = table_ref.shape[0]
+    lane = lax.broadcasted_iota(jnp.int32, (1, items), 1)
+    node = lax.broadcasted_iota(jnp.int32, (nodes, items), 0)
+    slot = lax.broadcasted_iota(jnp.int32, table_ref.shape, 1)
+    per = items // nodes
+    yd, xd = dest // SIDE, dest % SIDE
+
+    def step(t, carry):
+        y, x, code, ready, table = carry
+        ry, rx = (yd - y) & (SIDE - 1), (xd - x) & (SIDE - 1)
+        want = [
+            (rx == 1) | (rx == 2),
+            (rx == 3) | (rx == 2),
+            (ry == 1) | (ry == 2),
+            (ry == 3) | (ry == 2),
+        ]
+        want = [w.astype(F32) for w in want]
+        ways = want[0] + want[1] + want[2] + want[3]
+        share = jnp.where(ways > 0.0, 12.0 / jnp.maximum(ways, 1.0), 0.0)
+        left = (jnp.minimum(rx, SIDE - rx) + jnp.minimum(ry, SIDE - ry)).astype(F32)
+        here = ((node == y * SIDE + x) & (ready <= t)).astype(F32)
+        demand = [jnp.sum(here * (w * share), axis=1, keepdims=True) for w in want]
+        pull = sum(w * d for w, d in zip(want, demand))
+        rank = []
+        for a in range(4):
+            lower = 0.0
+            for b in range(4):
+                if b != a:
+                    under = demand[b] <= demand[a] if b < a else demand[b] < demand[a]
+                    lower = lower + under.astype(F32)
+            rank.append(lower)
+        free = here
+        code_f = code.astype(F32)
+        moves = [jnp.zeros((nodes, items), F32) for _ in range(4)]
+        for r in range(4):
+            turn = [(k == float(r)).astype(F32) for k in rank]
+            wanted = sum(w * u for w, u in zip(want, turn)) * free
+            own = sum(d * u for d, u in zip(demand, turn))
+            value = left * 192.0 + (pull - own)
+            key = jnp.where(wanted > 0.0, jnp.floor(value + 0.5) * 128.0 + (127.0 - code_f), -1.0)
+            best = jnp.max(key, axis=1, keepdims=True)
+            taken = ((key == best) & (best >= 0.0)).astype(F32)
+            free = free * (1.0 - taken)
+            picked = 127 - (best.astype(jnp.int32) & 127)
+            for d in range(4):
+                moves[d] = moves[d] + taken * turn[d]
+                here_now = (slot == t * 4 + d) & (turn[d] > 0.0) & (best >= 0.0)
+                table = jnp.where(here_now, picked, table)
+        gone = [jnp.sum(m, axis=0, keepdims=True).astype(jnp.int32) for m in moves]
+        x = (x + gone[0] - gone[1]) & (SIDE - 1)
+        y = (y + gone[2] - gone[3]) & (SIDE - 1)
+        for d in range(4):
+            code = jnp.where(gone[d] > 0, per + t * 4 + d, code)
+        ready = jnp.where(gone[0] + gone[1] + gone[2] + gone[3] > 0, t + 1 + DELAY, ready)
+        return y, x, code, ready, table
+
+    at = lane // per
+    zero = jnp.zeros((1, items), jnp.int32)
+    table = jnp.full(table_ref.shape, -1, jnp.int32)
+    y, x, code, _, table = lax.fori_loop(
+        0, most, step, (at // SIDE, at % SIDE, lane % per, zero, table)
+    )
+    table_ref[...] = table
+    final_ref[...] = jnp.where(y * SIDE + x == dest, code, 127)
+
+
+def schedule(dest, nodes):
+    return pl.pallas_call(
+        functools.partial(schedule_kernel, STEPS[-1]),
+        out_shape=[
+            jax.ShapeDtypeStruct((nodes, 128), jnp.int32),
+            jax.ShapeDtypeStruct(dest.shape, jnp.int32),
+        ],
+        compiler_params=params(),
+        cost_estimate=cost(10**7, 2**20),
+        name="schedule",
+    )(dest)
+
+
+def item_copies(code, pages, state, pool, received, target, sem):
+    local = state.shape[0]
+    rows = state.shape[1]
+    per = pages.shape[0] // local
+    tokens = pool.shape[1]
+
+    @pl.when((code >= 0) & (code < local))
+    def _():
+        pltpu.make_async_copy(state.at[code], target.at[pl.ds(0, rows)], sem).start()
+        for m in range(per):
+            pltpu.make_async_copy(
+                pool.at[pages[code * per + m]],
+                target.at[pl.ds(rows + m * tokens, tokens)],
+                sem,
+            ).start()
+
+    for b, source in enumerate(received):
+
+        @pl.when(code == local + b)
+        def _(source=source):
+            pltpu.make_async_copy(source, target, sem).start()
+
+
+def gather_kernel(t, codes, pages, state, pool, *refs):
+    received, targets, sem = refs[:-5], refs[-5:-1], refs[-1]
+    for d in range(4):
+        item_copies(codes[4 * t + d], pages, state, pool, received, targets[d], sem.at[d])
+    for d in range(4):
+
+        @pl.when(codes[4 * t + d] >= 0)
+        def _(d=d):
+            pltpu.make_async_copy(targets[d], targets[d], sem.at[d]).wait()
+
+
+def gather(t, codes, pages, state, pool, received):
+    rows = state.shape[1] + pages.shape[0] // state.shape[0] * pool.shape[1]
+    smem = pl.BlockSpec(memory_space=pltpu.SMEM)
+    hbm = pl.BlockSpec(memory_space=pltpu.HBM)
+    out = jax.ShapeDtypeStruct((rows, state.shape[2]), state.dtype)
+    return pl.pallas_call(
+        functools.partial(gather_kernel, t),
+        in_specs=[smem, smem] + [hbm] * (2 + len(received)),
+        out_specs=[hbm] * 4,
+        out_shape=[out] * 4,
+        scratch_shapes=[pltpu.SemaphoreType.DMA((4,))],
+        compiler_params=params(),
+        cost_estimate=cost(0, 16 * rows * state.shape[2]),
+        name="gather_step",
+    )(codes, pages, state, pool, *received)
+
+
+def shift(block, direction):
+    route = []
+    for n in range(lax.axis_size("sess")):
+        y, x = n // SIDE, n % SIDE
+        if direction < 2:
+            x = (x + 1 - 2 * direction) % SIDE
+        else:
+            y = (y + 1 - 2 * (direction - 2)) % SIDE
+        route.append((n, y * SIDE + x))
+    return lax.ppermute(block, "sess", route)
+
+
+def session_kernel(
+    codes, pages, prefix, base, c, b, scaled, cumul, gate, carry, queries, new, state, pool, *refs
+):
+    received, (gated, squares, fresh, out, held, sem) = refs[:-6], refs[-6:]
+    s = pl.program_id(0)
+    slots = pl.num_programs(0)
+    heads, width, depth = fresh.shape[1:]
+    rows = state.shape[1]
+
+    def fetch(at):
+        item_copies(codes[at], pages, state, pool, received, held.at[at % 2], sem.at[at % 2])
+
+    @pl.when(s == 0)
+    def _():
+        fetch(s)
+
+    @pl.when(s + 1 < slots)
+    def _():
+        fetch(s + 1)
+
+    now = held.at[s % 2]
+    pltpu.make_async_copy(now, now, sem.at[s % 2]).wait()
+    attend_step(now[rows:], queries[...], new[...], prefix[s], out)
+    mamba_step(
+        now[:rows].reshape(heads, width, depth),
+        base[...], c[...], b[...], scaled[...], cumul[0], gate[...], carry[0],
+        gated, squares, fresh,
+    )
+
+
+def sessions(
+    codes, pages, prefix, base, c, b, scaled, cumul, gate, carry, queries, new, state, pool,
+    received, shape,
+):
+    slots, tokens, heads = cumul.shape
+    total, width = base.shape
+
+    def own(block):
+        rest = (0,) * (len(block) - 1)
+        return pl.BlockSpec(block, lambda s: (s,) + rest)
+
+    smem = pl.BlockSpec(memory_space=pltpu.SMEM)
+    hbm = pl.BlockSpec(memory_space=pltpu.HBM)
+    rows = state.shape[1] + pages.shape[0] // slots * pool.shape[1]
+    return pl.pallas_call(
+        session_kernel,
+        grid=(slots,),
+        in_specs=[
+            smem,
+            smem,
+            smem,
+            own((tokens, width)),
+            own((tokens, NS)),
+            own((tokens, NS)),
+            own((tokens, width)),
+            own((1, tokens, heads)),
+            own((tokens, width)),
+            own((1, heads, NS)),
+            own((tokens, width)),
+            own((tokens, new.shape[1])),
+        ]
+        + [hbm] * (2 + len(received)),
+        out_specs=[
+            own((tokens, width)),
+            own((1, 1, tokens)),
+            own((1,) + shape[1:]),
+            own((tokens, width)),
+        ],
+        out_shape=[
+            jax.ShapeDtypeStruct((total, width), F32),
+            jax.ShapeDtypeStruct((slots, 1, tokens), F32),
+            jax.ShapeDtypeStruct(shape, BF16),
+            jax.ShapeDtypeStruct((total, width), BF16),
+        ],
+        scratch_shapes=[
+            pltpu.VMEM((2, rows, state.shape[2]), BF16),
+            pltpu.SemaphoreType.DMA((2,)),
+        ],
+        compiler_params=params(),
+        cost_estimate=cost(2 * 10**9, 32 * 2**20),
+        name="sessions",
+    )(
+        codes, pages, prefix, base, c, b, scaled, cumul, gate, carry, queries, new, state, pool,
+        *received,
+    )
+
+
+def shards(
+    mamba_x,
+    gate_z,
+    proj_bc,
+    step_raw,
+    step_bias,
+    decay_log,
+    skip_gain,
+    norm_gain,
+    state_cache,
+    cache_slot,
+    prefix_pages,
+    page_table,
+    queries,
+    appended_memory_pair,
+    key_value_pages,
+):
+    slots, heads = state_cache.shape[:2]
+    count = cache_slot.shape[0]
+    total = mamba_x.shape[0]
+    tokens = total // slots
+    me = lax.axis_index("sess")
+    names = jnp.arange(count, dtype=jnp.int32)
+    holds = (cache_slot[:, None] == names[None, :]).astype(jnp.int32)
+    dest = jnp.sum(holds * (names // slots)[:, None], axis=0, keepdims=True)
+    table, final = schedule(dest, count // slots)
+    needed = jnp.max(jnp.where(final < slots, 0, (final - slots) // 4 + 1))
+    done = jnp.max(final) < 127
+    choice = jnp.sum((needed > jnp.array(STEPS, jnp.int32)).astype(jnp.int32))
+    choice = jnp.where(done, choice, len(STEPS))
+    sends = lax.dynamic_index_in_dim(table, me, 0, keepdims=False)
+    local = jnp.arange(slots, dtype=jnp.int32)
+    at_home = (cache_slot[:, None] == (me * slots + local)[None, :]).astype(jnp.int32)
+    pages = jnp.sum(at_home[:, :, None] * page_table[:, None, :], axis=0).reshape(-1)
+    mine = lax.dynamic_slice_in_dim(cache_slot, me * slots, slots)
+    codes = jnp.sum((mine[:, None] == names[None, :]).astype(jnp.int32) * final, axis=1)
+
+    def run(steps, _):
+        pool = key_value_pages.reshape(key_value_pages.shape[:2] + (2 * HEAD_WIDTH,))
+        state = state_cache.reshape(slots, heads * P_SIZE, NS)
+        received = []
+        for t in range(steps):
+            ready = received[: 4 * max(0, t - DELAY)]
+            sent = gather(t, sends, pages, state, pool, ready)
+            received += [shift(block, d) for d, block in enumerate(sent)]
+
+        group = lax.axis_index("mp") * heads // (HM // G)
+        both = lax.dynamic_index_in_dim(proj_bc, group, axis=2, keepdims=False)
+        b, c = both[:, 0], both[:, 1]
+        delta = jax.nn.softplus(step_raw + step_bias[:, None]).reshape(heads, slots, tokens)
+        falloff = -jnp.exp(decay_log)[:, None, None] * delta
+        position = jnp.arange(tokens)
+        lower = (position[:, None] >= position[None, :]).astype(F32)
+        cumul = jnp.einsum("hsu,tu->hst", falloff, lower, precision=HIGHEST)
+        last = cumul[:, :, tokens - 1 :]
+        tail = (jnp.exp(last - cumul) * delta).transpose(1, 2, 0)
+        carry = jnp.exp(last[:, :, 0]).T[:, :, None]
+        carry = jnp.broadcast_to(carry, (slots, heads, NS))
+        rows = jnp.stack([cumul, delta], axis=0).transpose(2, 0, 1, 3)
+        rows = rows.reshape(slots, 2, heads * tokens)
+        cumul = cumul.transpose(1, 2, 0)
+        skip = jnp.repeat(skip_gain, P_SIZE)[None, :]
+        base, scaled = mamba_before(mamba_x, b, c, cumul, tail, rows, skip)
+        new = appended_memory_pair.reshape(total, 2 * HEAD_WIDTH)
+
+        gated, squares, fresh, out = sessions(
+            codes, pages, prefix_pages, base, c, b, scaled, cumul, gate_z, carry, queries, new,
+            state, pool, received, state_cache.shape,
+        )
+        squares = squares.reshape(total)
+        squares = squares + swapped(squares, "mp", 0)
+        scale = lax.rsqrt(squares / (HM // G * P_SIZE) + EPS)
+        mixed = (gated * scale[:, None] * norm_gain[None, :]).astype(BF16)
+        return mixed, fresh, out
+
+    def slow(_):
+        return padded(
+            mamba_x, gate_z, proj_bc, step_raw, step_bias, decay_log, skip_gain, norm_gain,
+            state_cache, cache_slot, prefix_pages, page_table, queries, appended_memory_pair,
+            key_value_pages,
+        )
+
+    return lax.switch(choice, [functools.partial(run, n) for n in STEPS] + [slow], 0)
 
 
 def solution(mesh):

time: 395 us -> 903 us (2.29)
  Pallas kernels: 0 us -> 675 us
  waiting for transfers between devices: 253 us -> 0.94 us
  starting transfers between devices: 15.7 us -> 149 us
  local copies, waits for them, and re-layouts: 67.6 us -> 22.9 us
  loops' own time: 0 us -> 38 us
  matrix products: 29.1 us -> 0.2 us
  other arithmetic: 27.4 us -> 10.5 us
    pallas_call x0 -> x14, Pallas kernels: none -> 675 us  [the longest x11 633 us: gather(): pl.pallas_call(functools.partial(gather_kernel, t), in_specs=[smem, smem]...]
    all_to_all x2 -> x0, waiting for transfers between devices: 253 us -> none  [the longest x1 216 us: shards(): lax.all_to_all(state_send, 'sess', split_axis=0, concat_axis=0, tiled=True)]
    ppermute x0 -> x44, starting transfers between devices: none -> 133 us  [shift(): return lax.ppermute(block, 'sess', route)]
    unnamed x0 -> x1, loops' own time: none -> 38 us
    gather x5 -> x0, local copies, waits for them, and re-layouts: 35.7 us -> none  [the longest x1 10.7 us: shards(): jnp.take(got_states.reshape((-1,) + state_cache.shape[1:]), picked, axis=0)]
    dot_general x7 -> x1, matrix products: 29.1 us -> 0.2 us  [run(): cumul = jnp.einsum('hsu,tu->hst', falloff, lower, precision=HIGHEST)]
    select_n x9 -> x2, other arithmetic: 20.8 us -> 0.15 us  [the longest x1 0.15 us: run(): jax.nn.softplus(step_raw + step_bias[:, None]).reshape(heads, slots, tokens)]
    ppermute x1, starting transfers between devices: 2.72 us -> 16.3 us  [swapped(): return lax.ppermute(block, axis, route)]
  transfers between devices with their start and end apart: 3 -> 45, of which waited for: 2 -> 1; matrix products, arithmetic and copies ran while one was open for 18% -> 1% of each run, Pallas kernels for 0% -> 63%
where the time goes in v1:
time: 903 us; the launch traced here: 898 us
  Pallas kernels  675 us (75%)
  starting transfers between devices  149 us (17%)
  loops' own time  38 us (4%)
  local copies, waits for them, and re-layouts  22.9 us (3%)
  other arithmetic  10.5 us (1%)
    pallas_call x11, Pallas kernels, gather(): pl.pallas_call(functools.partial(gather_kernel, t), in_specs=[smem, smem]...  633 us
    ppermute x44, starting transfers between devices, shift(): return lax.ppermute(block, 'sess', route)  133 us
    unnamed x1, loops' own time  38 us
    pallas_call x1, Pallas kernels, sessions(): pl.pallas_call(session_kernel, grid=(slots,), in_specs=[smem, smem, smem,...  22.8 us
  transfers between devices with their start and end apart: 45, of which 1 were waited for; matrix products, arithmetic and copies ran while one was open for 1% of the time, Pallas kernels for 63%

profile of v1, /device:TPU:1, one launch (start us, length us, event | category | flops | bytes accessed | tf_op | source)
XLA Modules:
  0.0 898.4 jit_solution(2798593436273464965)
XLA Ops:
  2.8 7.4 schedule.1
  14.1 883.0 %conditional.4 = (bf16[16,16,64,256]{3,2,1,0:T(8,128)(2,1)}, bf16[512,1024]{1,0:T(8,128)(2,1)}, bf16[512,1024]{1,0:T(8,128)(2,1)S(1)}) conditional(s32[]{:T(128)} %clamp.3, (bf16[512,2,4,256]{3,2,1,0:T(4,128)(2,1)}, f32[16]{0:T(128)}, f32[16]{0:T(128)}, f32[16,512]{1,0:T(8,128)}, f32[16]{0:T(128)}, ...), branch_computations={%region_6.7_spmd, %region_7.8_spmd, %region_8.9_spmd, %region_9.10... | conditional | flops 3004864512 | bytes 444222432
  24.4 4.5 reshape.429.pool
  29.5 81.2 %gather_step.70 = (bf16[1280,256]{1,0:T(8,128)(2,1)}, bf16[1280,256]{1,0:T(8,128)(2,1)}, bf16[1280,256]{1,0:T(8,128)(2,1)}, bf16[1280,256]{1,0:T(8,128)(2,1)}) custom-call(s32[128]{0:T(128)} %dynamic-slice_bitcast_fusion.4.codes, s32[64]{0:T(128)} %reshape.471.pages, bf16[16,1024,256]{2,1,0:T(8,128)(2,1)} %bitcast.294, bf16[64,64,256]{2,1,0:T(8,128)(2,1)} %reshape.429.pool), custom_call_target="tpu_custom_call" | custom-call | bytes 5242880 | tf_op jit(solution)/shard_map/cond/branch_1_fun/gather_step/pallas_call | solution.py:433
  117.0 81.2 %gather_step.71 = (bf16[1280,256]{1,0:T(8,128)(2,1)}, bf16[1280,256]{1,0:T(8,128)(2,1)}, bf16[1280,256]{1,0:T(8,128)(2,1)}, bf16[1280,256]{1,0:T(8,128)(2,1)}) custom-call(s32[128]{0:T(128)} %dynamic-slice_bitcast_fusion.4.codes, s32[64]{0:T(128)} %reshape.471.pages, bf16[16,1024,256]{2,1,0:T(8,128)(2,1)} %bitcast.295, bf16[64,64,256]{2,1,0:T(8,128)(2,1)} %reshape.429.pool), custom_call_target="tpu_custom_call" | custom-call | bytes 5242880 | tf_op jit(solution)/shard_map/cond/branch_1_fun/gather_step/pallas_call | solution.py:433
  204.6 81.2 %gather_step.72 = (bf16[1280,256]{1,0:T(8,128)(2,1)}, bf16[1280,256]{1,0:T(8,128)(2,1)}, bf16[1280,256]{1,0:T(8,128)(2,1)}, bf16[1280,256]{1,0:T(8,128)(2,1)}) custom-call(s32[128]{0:T(128)} %dynamic-slice_bitcast_fusion.4.codes, s32[64]{0:T(128)} %reshape.471.pages, bf16[16,1024,256]{2,1,0:T(8,128)(2,1)} %bitcast.296, bf16[64,64,256]{2,1,0:T(8,128)(2,1)} %reshape.429.pool, ...), custom_call_target="tpu_custom_call" | custom-call | bytes 5242880 | tf_op jit(solution)/shard_map/cond/branch_1_fun/gather_step/pallas_call | solution.py:433
  288.6 2.7 collective-permute-start.52
  292.1 81.2 %gather_step.73 = (bf16[1280,256]{1,0:T(8,128)(2,1)}, bf16[1280,256]{1,0:T(8,128)(2,1)}, bf16[1280,256]{1,0:T(8,128)(2,1)}, bf16[1280,256]{1,0:T(8,128)(2,1)}) custom-call(s32[128]{0:T(128)} %dynamic-slice_bitcast_fusion.4.codes, s32[64]{0:T(128)} %reshape.471.pages, bf16[16,1024,256]{2,1,0:T(8,128)(2,1)} %bitcast.297, bf16[64,64,256]{2,1,0:T(8,128)(2,1)} %reshape.429.pool, ...), custom_call_target="tpu_custom_call" | custom-call | bytes 5242880 | tf_op jit(solution)/shard_map/cond/branch_1_fun/gather_step/pallas_call | solution.py:433
  379.7 81.2 %gather_step.74 = (bf16[1280,256]{1,0:T(8,128)(2,1)}, bf16[1280,256]{1,0:T(8,128)(2,1)}, bf16[1280,256]{1,0:T(8,128)(2,1)}, bf16[1280,256]{1,0:T(8,128)(2,1)}) custom-call(s32[128]{0:T(128)} %dynamic-slice_bitcast_fusion.4.codes, s32[64]{0:T(128)} %reshape.471.pages, bf16[16,1024,256]{2,1,0:T(8,128)(2,1)} %bitcast.298, bf16[64,64,256]{2,1,0:T(8,128)(2,1)} %reshape.429.pool, ...), custom_call_target="tpu_custom_call" | custom-call | bytes 5242880 | tf_op jit(solution)/shard_map/cond/branch_1_fun/gather_step/pallas_call | solution.py:433
  467.3 81.3 %gather_step.75 = (bf16[1280,256]{1,0:T(8,128)(2,1)}, bf16[1280,256]{1,0:T(8,128)(2,1)}, bf16[1280,256]{1,0:T(8,128)(2,1)}, bf16[1280,256]{1,0:T(8,128)(2,1)}) custom-call(s32[128]{0:T(128)} %dynamic-slice_bitcast_fusion.4.codes, s32[64]{0:T(128)} %reshape.471.pages, bf16[16,1024,256]{2,1,0:T(8,128)(2,1)} %bitcast.299, bf16[64,64,256]{2,1,0:T(8,128)(2,1)} %reshape.429.pool, ...), custom_call_target="tpu_custom_call" | custom-call | bytes 5242880 | tf_op jit(solution)/shard_map/cond/branch_1_fun/gather_step/pallas_call | solution.py:433
  554.9 81.3 %gather_step.76 = (bf16[1280,256]{1,0:T(8,128)(2,1)}, bf16[1280,256]{1,0:T(8,128)(2,1)}, bf16[1280,256]{1,0:T(8,128)(2,1)}, bf16[1280,256]{1,0:T(8,128)(2,1)}) custom-call(s32[128]{0:T(128)} %dynamic-slice_bitcast_fusion.4.codes, s32[64]{0:T(128)} %reshape.471.pages, bf16[16,1024,256]{2,1,0:T(8,128)(2,1)} %bitcast.300, bf16[64,64,256]{2,1,0:T(8,128)(2,1)} %reshape.429.pool, ...), custom_call_target="tpu_custom_call" | custom-call | bytes 5242880 | tf_op jit(solution)/shard_map/cond/branch_1_fun/gather_step/pallas_call | solution.py:433
  638.9 3.0 collective-permute-start.68
  642.8 61.4 %gather_step.77 = (bf16[1280,256]{1,0:T(8,128)(2,1)}, bf16[1280,256]{1,0:T(8,128)(2,1)}, bf16[1280,256]{1,0:T(8,128)(2,1)}, bf16[1280,256]{1,0:T(8,128)(2,1)}) custom-call(s32[128]{0:T(128)} %dynamic-slice_bitcast_fusion.4.codes, s32[64]{0:T(128)} %reshape.471.pages, bf16[16,1024,256]{2,1,0:T(8,128)(2,1)} %bitcast.301, bf16[64,64,256]{2,1,0:T(8,128)(2,1)} %reshape.429.pool, ...), custom_call_target="tpu_custom_call" | custom-call | bytes 5242880 | tf_op jit(solution)/shard_map/cond/branch_1_fun/gather_step/pallas_call | solution.py:433
  704.5 2.7 collective-permute-start.70
  707.2 15.1 %collective-permute-start.71 = (bf16[1280,256]{1,0:T(8,128)(2,1)}, bf16[1280,256]{1,0:T(8,128)(2,1)S(1)}, u32[]{:S(2)}, u32[]{:S(2)}) collective-permute-start(bf16[1280,256]{1,0:T(8,128)(2,1)} %get-tuple-element.309), channel_id=1, source_target_pairs={{0,32},{8,40},{16,48},{24,56},{32,64},{40,72},{48,80},{56,88},{64,... | collective-permute-start | bytes 1966088 | tf_op jit(solution)/shard_map/cond/branch_1_fun/ppermute | solution.py:454
  722.3 5.3 collective-permute-start.72
  728.6 19.7 %collective-permute-start.73 = (bf16[1280,256]{1,0:T(8,128)(2,1)}, bf16[1280,256]{1,0:T(8,128)(2,1)}, u32[]{:S(2)}, u32[]{:S(2)}) collective-permute-start(bf16[1280,256]{1,0:T(8,128)(2,1)} %get-tuple-element.311), channel_id=1, source_target_pairs={{0,8},{8,16},{16,24},{24,0},{32,40},{40,48},{48,56},{56,32},{64,72... | collective-permute-start | bytes 1966088 | tf_op jit(solution)/shard_map/cond/branch_1_fun/ppermute | solution.py:454
  750.4 5.3 collective-permute-start.76
  759.4 14.8 %collective-permute-start.79 = (bf16[1280,256]{1,0:T(8,128)(2,1)}, bf16[1280,256]{1,0:T(8,128)(2,1)}, u32[]{:S(2)}, u32[]{:S(2)}) collective-permute-start(bf16[1280,256]{1,0:T(8,128)(2,1)} %get-tuple-element.317), channel_id=1, source_target_pairs={{0,32},{8,40},{16,48},{24,56},{32,64},{40,72},{48,80},{56,88},{64,... | collective-permute-start | bytes 1966088 | tf_op jit(solution)/shard_map/cond/branch_1_fun/ppermute | solution.py:454
  780.4 4.2 collective-permute-start.80
  789.0 20.5 %collective-permute-start.84 = (bf16[1280,256]{1,0:T(8,128)(2,1)}, bf16[1280,256]{1,0:T(8,128)(2,1)S(1)}, u32[]{:S(2)}, u32[]{:S(2)}) collective-permute-start(bf16[1280,256]{1,0:T(8,128)(2,1)} %get-tuple-element.322), channel_id=1, source_target_pairs={{0,96},{8,104},{16,112},{24,120},{32,0},{40,8},{48,16},{56,24},{64... | collective-permute-start | bytes 1966088 | tf_op jit(solution)/shard_map/cond/branch_1_fun/ppermute | solution.py:454
  811.0 11.5 %mamba_before.6 = (f32[512,1024]{1,0:T(8,128)}, bf16[512,1024]{1,0:T(8,128)(2,1)}) custom-call(bf16[512,1024]{1,0:T(8,128)(2,1)S(1)} %copy-done.215, bf16[512,256]{1,0:T(8,128)(2,1)} %get-tuple-element.1679.b_ref.b, bf16[512,256]{1,0:T(8,128)(2,1)} %get-tuple-element.1678.c_ref.c, f32[16,32,16]{2,1,0:T(8,128)} %bitcast.384, ...), custom_call_target="tpu_custom_call" | custom-call | flops 1000000000 | bytes 20971520 | tf_op jit(solution)/shard_map/cond/branch_1_fun/mamba_before/pallas_call | solution.py:242
  825.1 22.8 %sessions.6 = (f32[512,1024]{1,0:T(8,128)}, f32[16,1,32]{2,1,0:T(1,128)}, bf16[16,16,64,256]{3,2,1,0:T(8,128)(2,1)}, bf16[512,1024]{1,0:T(8,128)(2,1)}) custom-call(s32[16]{0:T(128)} %select_reduce_fusion.2.codes, s32[64]{0:T(128)} %reshape.471.pages, s32[16]{0:T(128)S(1)} %copy-done.275, f32[512,1024]{1,0:T(8,128)} %get-tuple-element.271.base, ...), custom_call_target="tpu_custom_call" | custom-call | flops 2000000000 | bytes 33554432 | tf_op jit(solution)/shard_map/cond/branch_1_fun/sessions/pallas_call | solution.py:501
  849.8 16.3 %collective-permute-start.85 = (f32[512]{0:T(512)S(1)}, f32[512]{0:T(512)S(1)}, u32[]{:S(2)}, u32[]{:S(2)}) collective-permute-start(f32[512]{0:T(512)S(1)} %reshape.430), channel_id=1, source_target_pairs={{0,1},{1,0},{2,3},{3,2},{4,5},{5,4},{6,7},{7,6},{8,9},{9,8},{10,11... | collective-permute-start | bytes 6152 | tf_op jit(solution)/shard_map/cond/branch_1_fun/ppermute | solution.py:42
  (217 shorter events, 72.4 us)
Async XLA Ops:
  110.7 87.6 %collective-permute-start.41 = (bf16[1280,256]{1,0:T(8,128)(2,1)}, bf16[1280,256]{1,0:T(8,128)(2,1)S(1)}, u32[]{:S(2)}, u32[]{:S(2)}) collective-permute-start(bf16[1280,256]{1,0:T(8,128)(2,1)} %get-tuple-element.279), channel_id=1, source_target_pairs={{0,8},{8,16},{16,24},{24,0},{32,40},{40,48},{48,56},{56,32},{64,72... | collective-permute-start | bytes 1966088 | tf_op jit(solution)/shard_map/cond/branch_1_fun/ppermute | solution.py:454
  112.8 88.2 %collective-permute-start.42 = (bf16[1280,256]{1,0:T(8,128)(2,1)}, bf16[1280,256]{1,0:T(8,128)(2,1)S(1)}, u32[]{:S(2)}, u32[]{:S(2)}) collective-permute-start(bf16[1280,256]{1,0:T(8,128)(2,1)} %get-tuple-element.280), channel_id=1, source_target_pairs={{0,24},{8,0},{16,8},{24,16},{32,56},{40,32},{48,40},{56,48},{64,88... | collective-permute-start | bytes 1966088 | tf_op jit(solution)/shard_map/cond/branch_1_fun/ppermute | solution.py:454
  115.6 88.1 %collective-permute-start.44 = (bf16[1280,256]{1,0:T(8,128)(2,1)}, bf16[1280,256]{1,0:T(8,128)(2,1)S(1)}, u32[]{:S(2)}, u32[]{:S(2)}) collective-permute-start(bf16[1280,256]{1,0:T(8,128)(2,1)} %get-tuple-element.282), channel_id=1, source_target_pairs={{0,96},{8,104},{16,112},{24,120},{32,0},{40,8},{48,16},{56,24},{64... | collective-permute-start | bytes 1966088 | tf_op jit(solution)/shard_map/cond/branch_1_fun/ppermute | solution.py:454
  198.2 87.7 %collective-permute-start.45 = (bf16[1280,256]{1,0:T(8,128)(2,1)}, bf16[1280,256]{1,0:T(8,128)(2,1)S(1)}, u32[]{:S(2)}, u32[]{:S(2)}) collective-permute-start(bf16[1280,256]{1,0:T(8,128)(2,1)} %get-tuple-element.283), channel_id=1, source_target_pairs={{0,8},{8,16},{16,24},{24,0},{32,40},{40,48},{48,56},{56,32},{64,72... | collective-permute-start | bytes 1966088 | tf_op jit(solution)/shard_map/cond/branch_1_fun/ppermute | solution.py:454
  198.3 90.2 %collective-permute-start.46 = (bf16[1280,256]{1,0:T(8,128)(2,1)}, bf16[1280,256]{1,0:T(8,128)(2,1)S(1)}, u32[]{:S(2)}, u32[]{:S(2)}) collective-permute-start(bf16[1280,256]{1,0:T(8,128)(2,1)} %get-tuple-element.284), channel_id=1, source_target_pairs={{0,24},{8,0},{16,8},{24,16},{32,56},{40,32},{48,40},{56,48},{64,88... | collective-permute-start | bytes 1966088 | tf_op jit(solution)/shard_map/cond/branch_1_fun/ppermute | solution.py:454
  201.0 87.6 %collective-permute-start.47 = (bf16[1280,256]{1,0:T(8,128)(2,1)}, bf16[1280,256]{1,0:T(8,128)(2,1)S(1)}, u32[]{:S(2)}, u32[]{:S(2)}) collective-permute-start(bf16[1280,256]{1,0:T(8,128)(2,1)} %get-tuple-element.285), channel_id=1, source_target_pairs={{0,32},{8,40},{16,48},{24,56},{32,64},{40,72},{48,80},{56,88},{64,... | collective-permute-start | bytes 1966088 | tf_op jit(solution)/shard_map/cond/branch_1_fun/ppermute | solution.py:454
  201.0 90.2 %collective-permute-start.48 = (bf16[1280,256]{1,0:T(8,128)(2,1)}, bf16[1280,256]{1,0:T(8,128)(2,1)S(1)}, u32[]{:S(2)}, u32[]{:S(2)}) collective-permute-start(bf16[1280,256]{1,0:T(8,128)(2,1)} %get-tuple-element.286), channel_id=1, source_target_pairs={{0,96},{8,104},{16,112},{24,120},{32,0},{40,8},{48,16},{56,24},{64... | collective-permute-start | bytes 1966088 | tf_op jit(solution)/shard_map/cond/branch_1_fun/ppermute | solution.py:454
  285.8 87.6 %collective-permute-start.49 = (bf16[1280,256]{1,0:T(8,128)(2,1)}, bf16[1280,256]{1,0:T(8,128)(2,1)S(1)}, u32[]{:S(2)}, u32[]{:S(2)}) collective-permute-start(bf16[1280,256]{1,0:T(8,128)(2,1)} %get-tuple-element.287), channel_id=1, source_target_pairs={{0,8},{8,16},{16,24},{24,0},{32,40},{40,48},{48,56},{56,32},{64,72... | collective-permute-start | bytes 1966088 | tf_op jit(solution)/shard_map/cond/branch_1_fun/ppermute | solution.py:454
  285.9 90.2 %collective-permute-start.50 = (bf16[1280,256]{1,0:T(8,128)(2,1)}, bf16[1280,256]{1,0:T(8,128)(2,1)S(1)}, u32[]{:S(2)}, u32[]{:S(2)}) collective-permute-start(bf16[1280,256]{1,0:T(8,128)(2,1)} %get-tuple-element.288), channel_id=1, source_target_pairs={{0,24},{8,0},{16,8},{24,16},{32,56},{40,32},{48,40},{56,48},{64,88... | collective-permute-start | bytes 1966088 | tf_op jit(solution)/shard_map/cond/branch_1_fun/ppermute | solution.py:454
  288.6 87.6 %collective-permute-start.51 = (bf16[1280,256]{1,0:T(8,128)(2,1)}, bf16[1280,256]{1,0:T(8,128)(2,1)S(1)}, u32[]{:S(2)}, u32[]{:S(2)}) collective-permute-start(bf16[1280,256]{1,0:T(8,128)(2,1)} %get-tuple-element.289), channel_id=1, source_target_pairs={{0,32},{8,40},{16,48},{24,56},{32,64},{40,72},{48,80},{56,88},{64,... | collective-permute-start | bytes 1966088 | tf_op jit(solution)/shard_map/cond/branch_1_fun/ppermute | solution.py:454
  288.6 90.2 %collective-permute-start.52 = (bf16[1280,256]{1,0:T(8,128)(2,1)}, bf16[1280,256]{1,0:T(8,128)(2,1)S(1)}, u32[]{:S(2)}, u32[]{:S(2)}) collective-permute-start(bf16[1280,256]{1,0:T(8,128)(2,1)} %get-tuple-element.290), channel_id=1, source_target_pairs={{0,96},{8,104},{16,112},{24,120},{32,0},{40,8},{48,16},{56,24},{64... | collective-permute-start | bytes 1966088 | tf_op jit(solution)/shard_map/cond/branch_1_fun/ppermute | solution.py:454
  373.4 87.7 %collective-permute-start.53 = (bf16[1280,256]{1,0:T(8,128)(2,1)}, bf16[1280,256]{1,0:T(8,128)(2,1)S(1)}, u32[]{:S(2)}, u32[]{:S(2)}) collective-permute-start(bf16[1280,256]{1,0:T(8,128)(2,1)} %get-tuple-element.291), channel_id=1, source_target_pairs={{0,8},{8,16},{16,24},{24,0},{32,40},{40,48},{48,56},{56,32},{64,72... | collective-permute-start | bytes 1966088 | tf_op jit(solution)/shard_map/cond/branch_1_fun/ppermute | solution.py:454
  373.5 90.2 %collective-permute-start.54 = (bf16[1280,256]{1,0:T(8,128)(2,1)}, bf16[1280,256]{1,0:T(8,128)(2,1)S(1)}, u32[]{:S(2)}, u32[]{:S(2)}) collective-permute-start(bf16[1280,256]{1,0:T(8,128)(2,1)} %get-tuple-element.292), channel_id=1, source_target_pairs={{0,24},{8,0},{16,8},{24,16},{32,56},{40,32},{48,40},{56,48},{64,88... | collective-permute-start | bytes 1966088 | tf_op jit(solution)/shard_map/cond/branch_1_fun/ppermute | solution.py:454
  376.1 87.6 %collective-permute-start.55 = (bf16[1280,256]{1,0:T(8,128)(2,1)}, bf16[1280,256]{1,0:T(8,128)(2,1)S(1)}, u32[]{:S(2)}, u32[]{:S(2)}) collective-permute-start(bf16[1280,256]{1,0:T(8,128)(2,1)} %get-tuple-element.293), channel_id=1, source_target_pairs={{0,32},{8,40},{16,48},{24,56},{32,64},{40,72},{48,80},{56,88},{64,... | collective-permute-start | bytes 1966088 | tf_op jit(solution)/shard_map/cond/branch_1_fun/ppermute | solution.py:454
  376.1 90.3 %collective-permute-start.56 = (bf16[1280,256]{1,0:T(8,128)(2,1)}, bf16[1280,256]{1,0:T(8,128)(2,1)S(1)}, u32[]{:S(2)}, u32[]{:S(2)}) collective-permute-start(bf16[1280,256]{1,0:T(8,128)(2,1)} %get-tuple-element.294), channel_id=1, source_target_pairs={{0,96},{8,104},{16,112},{24,120},{32,0},{40,8},{48,16},{56,24},{64... | collective-permute-start | bytes 1966088 | tf_op jit(solution)/shard_map/cond/branch_1_fun/ppermute | solution.py:454
  460.9 87.7 %collective-permute-start.57 = (bf16[1280,256]{1,0:T(8,128)(2,1)}, bf16[1280,256]{1,0:T(8,128)(2,1)S(1)}, u32[]{:S(2)}, u32[]{:S(2)}) collective-permute-start(bf16[1280,256]{1,0:T(8,128)(2,1)} %get-tuple-element.295), channel_id=1, source_target_pairs={{0,8},{8,16},{16,24},{24,0},{32,40},{40,48},{48,56},{56,32},{64,72... | collective-permute-start | bytes 1966088 | tf_op jit(solution)/shard_map/cond/branch_1_fun/ppermute | solution.py:454
  461.1 90.3 %collective-permute-start.58 = (bf16[1280,256]{1,0:T(8,128)(2,1)}, bf16[1280,256]{1,0:T(8,128)(2,1)S(1)}, u32[]{:S(2)}, u32[]{:S(2)}) collective-permute-start(bf16[1280,256]{1,0:T(8,128)(2,1)} %get-tuple-element.296), channel_id=1, source_target_pairs={{0,24},{8,0},{16,8},{24,16},{32,56},{40,32},{48,40},{56,48},{64,88... | collective-permute-start | bytes 1966088 | tf_op jit(solution)/shard_map/cond/branch_1_fun/ppermute | solution.py:454
  463.7 87.6 %collective-permute-start.59 = (bf16[1280,256]{1,0:T(8,128)(2,1)}, bf16[1280,256]{1,0:T(8,128)(2,1)S(1)}, u32[]{:S(2)}, u32[]{:S(2)}) collective-permute-start(bf16[1280,256]{1,0:T(8,128)(2,1)} %get-tuple-element.297), channel_id=1, source_target_pairs={{0,32},{8,40},{16,48},{24,56},{32,64},{40,72},{48,80},{56,88},{64,... | collective-permute-start | bytes 1966088 | tf_op jit(solution)/shard_map/cond/branch_1_fun/ppermute | solution.py:454
  463.7 90.3 %collective-permute-start.60 = (bf16[1280,256]{1,0:T(8,128)(2,1)}, bf16[1280,256]{1,0:T(8,128)(2,1)S(1)}, u32[]{:S(2)}, u32[]{:S(2)}) collective-permute-start(bf16[1280,256]{1,0:T(8,128)(2,1)} %get-tuple-element.298), channel_id=1, source_target_pairs={{0,96},{8,104},{16,112},{24,120},{32,0},{40,8},{48,16},{56,24},{64... | collective-permute-start | bytes 1966088 | tf_op jit(solution)/shard_map/cond/branch_1_fun/ppermute | solution.py:454
  548.6 87.7 %collective-permute-start.61 = (bf16[1280,256]{1,0:T(8,128)(2,1)}, bf16[1280,256]{1,0:T(8,128)(2,1)S(1)}, u32[]{:S(2)}, u32[]{:S(2)}) collective-permute-start(bf16[1280,256]{1,0:T(8,128)(2,1)} %get-tuple-element.299), channel_id=1, source_target_pairs={{0,8},{8,16},{16,24},{24,0},{32,40},{40,48},{48,56},{56,32},{64,72... | collective-permute-start | bytes 1966088 | tf_op jit(solution)/shard_map/cond/branch_1_fun/ppermute | solution.py:454
  548.7 90.2 %collective-permute-start.62 = (bf16[1280,256]{1,0:T(8,128)(2,1)}, bf16[1280,256]{1,0:T(8,128)(2,1)S(1)}, u32[]{:S(2)}, u32[]{:S(2)}) collective-permute-start(bf16[1280,256]{1,0:T(8,128)(2,1)} %get-tuple-element.300), channel_id=1, source_target_pairs={{0,24},{8,0},{16,8},{24,16},{32,56},{40,32},{48,40},{56,48},{64,88... | collective-permute-start | bytes 1966088 | tf_op jit(solution)/shard_map/cond/branch_1_fun/ppermute | solution.py:454
  551.3 87.6 %collective-permute-start.63 = (bf16[1280,256]{1,0:T(8,128)(2,1)}, bf16[1280,256]{1,0:T(8,128)(2,1)S(1)}, u32[]{:S(2)}, u32[]{:S(2)}) collective-permute-start(bf16[1280,256]{1,0:T(8,128)(2,1)} %get-tuple-element.301), channel_id=1, source_target_pairs={{0,32},{8,40},{16,48},{24,56},{32,64},{40,72},{48,80},{56,88},{64,... | collective-permute-start | bytes 1966088 | tf_op jit(solution)/shard_map/cond/branch_1_fun/ppermute | solution.py:454
  551.4 90.6 %collective-permute-start.64 = (bf16[1280,256]{1,0:T(8,128)(2,1)}, bf16[1280,256]{1,0:T(8,128)(2,1)S(1)}, u32[]{:S(2)}, u32[]{:S(2)}) collective-permute-start(bf16[1280,256]{1,0:T(8,128)(2,1)} %get-tuple-element.302), channel_id=1, source_target_pairs={{0,96},{8,104},{16,112},{24,120},{32,0},{40,8},{48,16},{56,24},{64... | collective-permute-start | bytes 1966088 | tf_op jit(solution)/shard_map/cond/branch_1_fun/ppermute | solution.py:454
  638.9 88.7 %collective-permute-start.68 = (bf16[1280,256]{1,0:T(8,128)(2,1)}, bf16[1280,256]{1,0:T(8,128)(2,1)}, u32[]{:S(2)}, u32[]{:S(2)}) collective-permute-start(bf16[1280,256]{1,0:T(8,128)(2,1)} %get-tuple-element.306), channel_id=1, source_target_pairs={{0,96},{8,104},{16,112},{24,120},{32,0},{40,8},{48,16},{56,24},{64... | collective-permute-start | bytes 1966088 | tf_op jit(solution)/shard_map/cond/branch_1_fun/ppermute | solution.py:454
  (68 other events, 1415.1 us)

commit v2 on v1

v2 whole, which is shorter than its diff:
```python
import functools

import jax
import jax.numpy as jnp
from jax import lax
from jax.experimental import pallas as pl
from jax.experimental.pallas import tpu as pltpu
from jax.sharding import PartitionSpec as P

HM = 128
P_SIZE = 64
NS = 256
G = 4
HEAD_WIDTH = 128
PAGE_TOKENS = 64
EPS = 1e-05

STEPS = (10, 14)
EARLY = 1
LOST = 127
DELAY = 1
SIDE = 4
HIGHEST = lax.Precision.HIGHEST
F32 = jnp.float32
BF16 = jnp.bfloat16


def params():
    return pltpu.CompilerParams(vmem_limit_bytes=56 * 1024 * 1024)


def cost(flops, moved):
    return pl.CostEstimate(flops=flops, bytes_accessed=moved, transcendentals=0)


def swapped(block, axis, stride):
    count = lax.axis_size(axis)
    route = []
    for low in range(count):
        high = low | 1 << stride
        if high != low and high < count:
            route += [(low, high), (high, low)]
    return lax.ppermute(block, axis, route)


def dot(a, b, dims, precision=None):
    return lax.dot_general(
        a, b, ((dims[:1], dims[1:]), ((), ())), precision=precision, preferred_element_type=F32
    )


def spread_matrix(heads, lanes):
    row = lax.broadcasted_iota(jnp.int32, (heads, heads * lanes), 0)
    column = lax.broadcasted_iota(jnp.int32, (heads, heads * lanes), 1)
    return (row == column // lanes).astype(BF16)


def spread(columns, lanes):
    parts = []
    for _ in range(3):
        parts.append(columns.astype(BF16))
        columns = columns - parts[-1].astype(F32)
    matrix = spread_matrix(columns.shape[1], lanes)
    return dot(jnp.concatenate(parts, axis=1), jnp.concatenate([matrix] * 3, axis=0), (1, 0))


def before_kernel(x_ref, b_ref, c_ref, cumul_ref, tail_ref, row_ref, skip_ref, base, scaled):
    heads = cumul_ref.shape[2]
    tokens = x_ref.shape[0]
    quad = 4
    x = x_ref[...]
    inner = dot(c_ref[...], b_ref[...], (1, 1))
    at_t = spread(cumul_ref[0], tokens)
    row = lax.broadcasted_iota(jnp.int32, at_t.shape, 0)
    column = lax.broadcasted_iota(jnp.int32, at_t.shape, 1)
    causal = row >= column % tokens
    gap = at_t - row_ref[0, 0:1]
    decay = jnp.where(causal, jnp.exp(jnp.where(causal, gap, 0.0)), 0.0)
    inner = jnp.concatenate([inner] * heads, axis=1)
    weights = (inner * decay * row_ref[0, 1:2]).astype(BF16)
    own_row = lax.broadcasted_iota(jnp.int32, (quad * tokens, quad * P_SIZE), 0) // tokens
    own_column = lax.broadcasted_iota(jnp.int32, (quad * tokens, quad * P_SIZE), 1) // P_SIZE
    own = own_row == own_column
    for q in range(heads // quad):
        lanes = slice(q * quad * P_SIZE, (q + 1) * quad * P_SIZE)
        values = x[:, lanes].astype(F32)
        stacked = jnp.where(own, jnp.concatenate([values] * quad, axis=0), 0.0).astype(BF16)
        part = weights[:, q * quad * tokens : (q + 1) * quad * tokens]
        base[:, lanes] = dot(part, stacked, (1, 0)) + skip_ref[:, lanes] * values
    scaled[...] = (x.astype(F32) * spread(tail_ref[0], P_SIZE)).astype(BF16)


def mamba_before(x, b, c, cumul, tail, rows, skip):
    total, width = x.shape
    slots, tokens, heads = cumul.shape
    per = lambda shape: pl.BlockSpec(shape, lambda s: (s,) + (0,) * (len(shape) - 1))
    return pl.pallas_call(
        before_kernel,
        grid=(slots,),
        in_specs=[
            per((tokens, width)),
            per((tokens, NS)),
            per((tokens, NS)),
            per((1, tokens, heads)),
            per((1, tokens, heads)),
            per((1, 2, heads * tokens)),
            pl.BlockSpec((1, width), lambda s: (0, 0)),
        ],
        out_specs=[per((tokens, width)), per((tokens, width))],
        out_shape=[
            jax.ShapeDtypeStruct((total, width), F32),
            jax.ShapeDtypeStruct((total, width), BF16),
        ],
        compiler_params=params(),
        cost_estimate=cost(10**9, 20 * 2**20),
        name="mamba_before",
    )(x, b, c, cumul, tail, rows, skip)


def mamba_step(state, base, c, b, scaled, cumul, gate, carry, gated, squares, fresh):
    heads = state.shape[0]
    carried = dot(c, state.reshape(heads * P_SIZE, NS), (1, 1))
    out = base + carried * spread(jnp.exp(cumul), P_SIZE)
    gate = gate.astype(F32)
    value = out * (gate / (1.0 + jnp.exp(-gate)))
    gated[...] = value
    ones = jnp.ones((8, value.shape[1]), F32)
    squares[0] = dot(ones, value * value, (1, 1), HIGHEST)[0:1]
    local = dot(scaled, b, (0, 0))
    for h in range(heads):
        rows = slice(h * P_SIZE, (h + 1) * P_SIZE)
        fresh[0, h] = (carry[h : h + 1] * state[h].astype(F32) + local[rows]).astype(BF16)


def attend_step(pages, queries, new, prefix, out):
    kept = pages.shape[0]
    tokens = queries.shape[0]
    heads = queries.shape[1] // HEAD_WIDTH
    q = jnp.concatenate(
        [queries[:, g * HEAD_WIDTH : (g + 1) * HEAD_WIDTH] for g in range(heads)], axis=0
    )
    factor = HEAD_WIDTH ** (-0.5)
    old_scores = dot(q, pages[:, :HEAD_WIDTH], (1, 1)) * factor
    new_scores = dot(q, new[:, :HEAD_WIDTH], (1, 1)) * factor
    column = lax.broadcasted_iota(jnp.int32, old_scores.shape, 1)
    old_scores = jnp.where(column < prefix * PAGE_TOKENS, old_scores, -jnp.inf)
    row = lax.broadcasted_iota(jnp.int32, new_scores.shape, 0) % tokens
    column = lax.broadcasted_iota(jnp.int32, new_scores.shape, 1)
    new_scores = jnp.where(column <= row, new_scores, -jnp.inf)
    peak = jnp.maximum(
        jnp.max(old_scores, axis=1, keepdims=True), jnp.max(new_scores, axis=1, keepdims=True)
    )
    old_expo = jnp.exp(old_scores - peak)
    new_expo = jnp.exp(new_scores - peak)
    total = jnp.sum(old_expo, axis=1, keepdims=True) + jnp.sum(new_expo, axis=1, keepdims=True)
    old_probs = (old_expo / total).astype(BF16)
    new_probs = (new_expo / total).astype(BF16)
    mixed = dot(old_probs, pages[:, HEAD_WIDTH:], (1, 0)) + dot(
        new_probs, new[:, HEAD_WIDTH:], (1, 0)
    )
    for g in range(heads):
        out[:, g * HEAD_WIDTH : (g + 1) * HEAD_WIDTH] = mixed[
            g * tokens : (g + 1) * tokens
        ].astype(BF16)


def schedule_kernel(first, last, dest_ref, *refs):
    old_table, old_items, table_ref, items_ref = refs if len(refs) == 4 else (None, None) + refs
    dest = dest_ref[...]
    items = dest.shape[1]
    nodes = table_ref.shape[0]
    lane = lax.broadcasted_iota(jnp.int32, (1, items), 1)
    node = lax.broadcasted_iota(jnp.int32, (nodes, items), 0)
    slot = lax.broadcasted_iota(jnp.int32, table_ref.shape, 1)
    per = items // nodes
    yd, xd = dest // SIDE, dest % SIDE

    def step(t, carry):
        y, x, code, ready, table = carry
        ry, rx = (yd - y) & (SIDE - 1), (xd - x) & (SIDE - 1)
        want = [
            (rx == 1) | (rx == 2),
            (rx == 3) | (rx == 2),
            (ry == 1) | (ry == 2),
            (ry == 3) | (ry == 2),
        ]
        want = [w.astype(F32) for w in want]
        ways = want[0] + want[1] + want[2] + want[3]
        share = jnp.where(ways > 0.0, 12.0 / jnp.maximum(ways, 1.0), 0.0)
        left = (jnp.minimum(rx, SIDE - rx) + jnp.minimum(ry, SIDE - ry)).astype(F32)
        here = ((node == y * SIDE + x) & (ready <= t)).astype(F32)
        demand = [jnp.sum(here * (w * share), axis=1, keepdims=True) for w in want]
        pull = sum(w * d for w, d in zip(want, demand))
        rank = []
        for a in range(4):
            lower = 0.0
            for b in range(4):
                if b != a:
                    under = demand[b] <= demand[a] if b < a else demand[b] < demand[a]
                    lower = lower + under.astype(F32)
            rank.append(lower)
        free = here
        code_f = code.astype(F32)
        moves = [jnp.zeros((nodes, items), F32) for _ in range(4)]
        for r in range(4):
            turn = [(k == float(r)).astype(F32) for k in rank]
            wanted = sum(w * u for w, u in zip(want, turn)) * free
            own = sum(d * u for d, u in zip(demand, turn))
            value = left * 192.0 + (pull - own)
            key = jnp.where(wanted > 0.0, jnp.floor(value + 0.5) * 128.0 + (127.0 - code_f), -1.0)
            best = jnp.max(key, axis=1, keepdims=True)
            taken = ((key == best) & (best >= 0.0)).astype(F32)
            free = free * (1.0 - taken)
            picked = 127 - (best.astype(jnp.int32) & 127)
            for d in range(4):
                moves[d] = moves[d] + taken * turn[d]
                here_now = (slot == t * 4 + d) & (turn[d] > 0.0) & (best >= 0.0)
                table = jnp.where(here_now, picked, table)
        gone = [jnp.sum(m, axis=0, keepdims=True).astype(jnp.int32) for m in moves]
        x = (x + gone[0] - gone[1]) & (SIDE - 1)
        y = (y + gone[2] - gone[3]) & (SIDE - 1)
        for d in range(4):
            code = jnp.where(gone[d] > 0, per + t * 4 + d, code)
        ready = jnp.where(gone[0] + gone[1] + gone[2] + gone[3] > 0, t + 1 + DELAY, ready)
        return y, x, code, ready, table

    if old_table is None:
        at = lane // per
        state = (at // SIDE, at % SIDE, lane % per, jnp.zeros((1, items), jnp.int32))
        table = jnp.full(table_ref.shape, -1, jnp.int32)
    else:
        state = tuple(old_items[n : n + 1] for n in range(4))
        table = old_table[...]
    y, x, code, ready, table = lax.fori_loop(first, last, step, state + (table,))
    table_ref[...] = table
    for n, row in enumerate((y, x, code, ready)):
        items_ref[n : n + 1] = row
    items_ref[4:5] = y * SIDE + x
    items_ref[5:6] = jnp.where(y * SIDE + x == dest, code, LOST)
    items_ref[6:8] = jnp.zeros((2, items), jnp.int32)


def schedule(dest, nodes, first, last, before=()):
    return pl.pallas_call(
        functools.partial(schedule_kernel, first, last),
        out_shape=[
            jax.ShapeDtypeStruct((nodes, 128), jnp.int32),
            jax.ShapeDtypeStruct((8, dest.shape[1]), jnp.int32),
        ],
        compiler_params=params(),
        cost_estimate=cost(10**7, 2**20),
        name="schedule",
    )(dest, *before)


def item_copies(code, pages, state, pool, target, sem):
    local = state.shape[0]
    rows = state.shape[1]
    per = pages.shape[0] // local
    tokens = pool.shape[1]

    @pl.when((code >= 0) & (code < local))
    def _():
        pltpu.make_async_copy(state.at[code], target.at[pl.ds(0, rows)], sem).start()
        for m in range(per):
            pltpu.make_async_copy(
                pool.at[pages[code * per + m]],
                target.at[pl.ds(rows + m * tokens, tokens)],
                sem,
            ).start()


def gather_kernel(t, codes, pages, state, pool, previous, *refs):
    received, targets, (held, sem, out_sem) = refs[:-7], refs[-7:-3], refs[-3:]
    local = state.shape[0]
    wanted = [codes[4 * t + d] for d in range(4)]

    def load(d, carry):
        item_copies(codes[4 * t + d], pages, state, pool, held.at[d], sem.at[d])
        return carry

    lax.fori_loop(0, 4, load, 0)
    for b, source in enumerate(received):
        hits = [(code == local + b).astype(jnp.int32) for code in wanted]

        @pl.when(hits[0] + hits[1] + hits[2] + hits[3] > 0)
        def _(source=source, d=hits[1] + 2 * hits[2] + 3 * hits[3]):
            pltpu.make_async_copy(source, held.at[d], sem.at[d]).start()

    def store(d):
        return pltpu.make_async_copy(held.at[d], targets[d], out_sem.at[d])

    for d in range(4):

        @pl.when(wanted[d] >= 0)
        def _(d=d):
            pltpu.make_async_copy(held.at[d], held.at[d], sem.at[d]).wait()
            store(d).start()

    for d in range(4):

        @pl.when(wanted[d] >= 0)
        def _(d=d):
            store(d).wait()


def gather(t, codes, pages, state, pool, previous, received):
    rows = state.shape[1] + pages.shape[0] // state.shape[0] * pool.shape[1]
    smem = pl.BlockSpec(memory_space=pltpu.SMEM)
    anywhere = pl.BlockSpec(memory_space=pl.ANY)
    out = jax.ShapeDtypeStruct((rows, state.shape[2]), state.dtype)
    return pl.pallas_call(
        functools.partial(gather_kernel, t),
        in_specs=[smem, smem] + [anywhere] * (3 + len(received)),
        out_specs=[pl.BlockSpec(memory_space=pltpu.HBM)] * 4,
        out_shape=[out] * 4,
        scratch_shapes=[
            pltpu.VMEM((4, rows, state.shape[2]), state.dtype),
            pltpu.SemaphoreType.DMA((4,)),
            pltpu.SemaphoreType.DMA((4,)),
        ],
        compiler_params=params(),
        cost_estimate=cost(0, 16 * rows * state.shape[2]),
        name="gather_step",
    )(codes, pages, state, pool, previous, *received)


def blank_kernel(*refs):
    pass


def blank(shapes):
    hbm = pl.BlockSpec(memory_space=pltpu.HBM)
    return pl.pallas_call(
        blank_kernel,
        out_specs=[hbm] * len(shapes),
        out_shape=shapes,
        compiler_params=params(),
        name="blank",
    )()


def shift(block, direction):
    route = []
    for n in range(lax.axis_size("sess")):
        y, x = n // SIDE, n % SIDE
        if direction < 2:
            x = (x + 1 - 2 * direction) % SIDE
        else:
            y = (y + 1 - 2 * (direction - 2)) % SIDE
        route.append((n, y * SIDE + x))
    return lax.ppermute(block, "sess", route)


def session_kernel(
    codes, pages, prefix, base, c, b, scaled, cumul, gate, carry, queries, new, state, pool, *refs
):
    received, late, (gated, squares, fresh, out, held, sem) = refs[:-7], refs[-7], refs[-6:]
    at = pl.program_id(0)
    slots = pl.num_programs(0) - 1
    heads, width, depth = fresh.shape[1:]
    rows = state.shape[1]

    @pl.when(at < slots)
    def _():
        code = codes[at]
        target, done = held.at[at % 2], sem.at[at % 2]
        item_copies(code, pages, state, pool, target, done)
        for b, source in enumerate(received):

            @pl.when(code == state.shape[0] + b)
            def _(source=source):
                pltpu.make_async_copy(source, target, done).start()

        @pl.when(code == LOST)
        def _():
            pltpu.make_async_copy(late.at[at], target, done).start()

    @pl.when(at > 0)
    def _():
        s = at - 1
        now = held.at[s % 2]
        pltpu.make_async_copy(now, now, sem.at[s % 2]).wait()
        attend_step(now[rows:], queries[...], new[...], prefix[s], out)
        mamba_step(
            now[:rows].reshape(heads, width, depth),
            base[...], c[...], b[...], scaled[...], cumul[0], gate[...], carry[0],
            gated, squares, fresh,
        )


def sessions(
    codes, pages, prefix, base, c, b, scaled, cumul, gate, carry, queries, new, state, pool,
    received, late, shape,
):
    slots, tokens, heads = cumul.shape
    total, width = base.shape

    def own(block):
        rest = (0,) * (len(block) - 1)
        return pl.BlockSpec(block, lambda s: (jnp.maximum(s - 1, 0),) + rest)

    smem = pl.BlockSpec(memory_space=pltpu.SMEM)
    anywhere = pl.BlockSpec(memory_space=pl.ANY)
    return pl.pallas_call(
        session_kernel,
        grid=(slots + 1,),
        in_specs=[
            smem,
            smem,
            smem,
            own((tokens, width)),
            own((tokens, NS)),
            own((tokens, NS)),
            own((tokens, width)),
            own((1, tokens, heads)),
            own((tokens, width)),
            own((1, heads, NS)),
            own((tokens, width)),
            own((tokens, new.shape[1])),
        ]
        + [anywhere] * (3 + len(received)),
        out_specs=[
            own((tokens, width)),
            own((1, 1, tokens)),
            own((1,) + shape[1:]),
            own((tokens, width)),
        ],
        out_shape=[
            jax.ShapeDtypeStruct((total, width), F32),
            jax.ShapeDtypeStruct((slots, 1, tokens), F32),
            jax.ShapeDtypeStruct(shape, BF16),
            jax.ShapeDtypeStruct((total, width), BF16),
        ],
        scratch_shapes=[
            pltpu.VMEM((2,) + late.shape[1:], BF16),
            pltpu.SemaphoreType.DMA((2,)),
        ],
        compiler_params=params(),
        cost_estimate=cost(2 * 10**9, 32 * 2**20),
        name="sessions",
    )(
        codes, pages, prefix, base, c, b, scaled, cumul, gate, carry, queries, new, state, pool,
        *received, late,
    )


def shards(
    mamba_x,
    gate_z,
    proj_bc,
    step_raw,
    step_bias,
    decay_log,
    skip_gain,
    norm_gain,
    state_cache,
    cache_slot,
    prefix_pages,
    page_table,
    queries,
    appended_memory_pair,
    key_value_pages,
):
    slots, heads = state_cache.shape[:2]
    count = cache_slot.shape[0]
    total = mamba_x.shape[0]
    tokens = total // slots
    me = lax.axis_index("sess")
    nodes = count // slots
    names = jnp.arange(count, dtype=jnp.int32)
    holds = (cache_slot[:, None] == names[None, :]).astype(jnp.int32)
    session = jnp.sum(holds * names[:, None], axis=0, keepdims=True)
    dest = session // slots

    def row(table):
        return lax.dynamic_index_in_dim(table, me, 0, keepdims=False)

    early = schedule(dest, nodes, 0, EARLY)
    table, items = schedule(dest, nodes, EARLY, STEPS[1], early)
    early_sends, sends = row(early[0]), row(table)
    final = items[5]
    needed = jnp.max(jnp.where(items[2] < slots, 0, (items[2] - slots) // 4 + 1))
    local = jnp.arange(slots, dtype=jnp.int32)
    at_home = (cache_slot[:, None] == (me * slots + local)[None, :]).astype(jnp.int32)
    pages = jnp.sum(at_home[:, :, None] * page_table[:, None, :], axis=0).reshape(-1)
    mine = lax.dynamic_slice_in_dim(cache_slot, me * slots, slots)
    codes = jnp.sum((mine[:, None] == names[None, :]).astype(jnp.int32) * final, axis=1)

    pool = key_value_pages.reshape(key_value_pages.shape[:2] + (2 * HEAD_WIDTH,))
    state = state_cache.reshape(slots, heads * P_SIZE, NS)
    item = (heads * P_SIZE + page_table.shape[1] * PAGE_TOKENS, NS)

    def step(t, sent, received):
        ready = received[: 4 * max(0, t - DELAY)]
        plan = early_sends if t < EARLY else sends
        sent = gather(t, plan, pages, state, pool, sent[0], ready)
        return sent, received + [shift(block, d) for d, block in enumerate(sent)]

    sent, received = [pool], []
    for t in range(STEPS[0]):
        sent, received = step(t, sent, received)

    def deliver(received, held):
        def body(carry):
            left, held = carry
            c = jnp.argmax(left)
            code = items[2][c]
            block = gather(0, jnp.stack([code, -1, -1, -1]), pages, state, pool, pool, received)[0]
            to = session[0][c]
            place = to % slots
            old = lax.dynamic_index_in_dim(held, place, 0, keepdims=False)
            ring = [(n, (n + 1) % nodes) for n in range(nodes)]

            def turn(r, carry):
                block, kept = carry
                block = lax.ppermute(block, "sess", ring)
                mine = (to // slots == me) & ((items[4][c] + r) % nodes == me)
                return block, jnp.where(mine, block, kept)

            block = lax.fori_loop(1, nodes, turn, (block, old))[1]
            held = lax.dynamic_update_index_in_dim(held, block, place, 0)
            return left.at[c].set(0), held

        left = (final == LOST).astype(jnp.int32)
        return lax.while_loop(lambda carry: jnp.max(carry[0]) > 0, body, (left, held))[1]

    def shapes(t):
        kinds = [jax.ShapeDtypeStruct(item, BF16)] * (4 * (STEPS[1] - t))
        return kinds + [jax.ShapeDtypeStruct((slots,) + item, BF16)]

    def late_steps(t, received):
        if t == STEPS[1]:
            return [deliver(received, blank(shapes(t))[0])]

        def more(_):
            after = step(t, [pool], received)[1]
            return after[4 * t :] + late_steps(t + 1, after)

        return list(lax.cond(needed > t, more, lambda _: list(blank(shapes(t))), 0))

    rest = late_steps(STEPS[0], received)
    received, late = received + rest[:-1], rest[-1]

    group = lax.axis_index("mp") * heads // (HM // G)
    both = lax.dynamic_index_in_dim(proj_bc, group, axis=2, keepdims=False)
    b, c = both[:, 0], both[:, 1]
    delta = jax.nn.softplus(step_raw + step_bias[:, None]).reshape(heads, slots, tokens)
    falloff = -jnp.exp(decay_log)[:, None, None] * delta
    position = jnp.arange(tokens)
    lower = (position[:, None] >= position[None, :]).astype(F32)
    cumul = jnp.einsum("hsu,tu->hst", falloff, lower, precision=HIGHEST)
    last = cumul[:, :, tokens - 1 :]
    tail = (jnp.exp(last - cumul) * delta).transpose(1, 2, 0)
    carry = jnp.exp(last[:, :, 0]).T[:, :, None]
    carry = jnp.broadcast_to(carry, (slots, heads, NS))
    rows = jnp.stack([cumul, delta], axis=0).transpose(2, 0, 1, 3)
    rows = rows.reshape(slots, 2, heads * tokens)
    cumul = cumul.transpose(1, 2, 0)
    skip = jnp.repeat(skip_gain, P_SIZE)[None, :]
    base, scaled = mamba_before(mamba_x, b, c, cumul, tail, rows, skip)
    new = appended_memory_pair.reshape(total, 2 * HEAD_WIDTH)

    gated, squares, fresh, out = sessions(
        codes, pages, prefix_pages, base, c, b, scaled, cumul, gate_z, carry, queries, new,
        state, pool, received, late, state_cache.shape,
    )
    squares = squares.reshape(total)
    squares = squares + swapped(squares, "mp", 0)
    scale = lax.rsqrt(squares / (HM // G * P_SIZE) + EPS)
    mixed = (gated * scale[:, None] * norm_gain[None, :]).astype(BF16)
    return mixed, fresh, out


def solution(mesh):
    return jax.shard_map(
        shards,
        mesh=mesh,
        in_specs=(
            P("sess", "mp"),
            P("sess", "mp"),
            P("sess", None, None, None),
            P("mp", "sess"),
            P("mp"),
            P("mp"),
            P("mp"),
            P("mp"),
            P("sess", "mp", None, None),
            P(),
            P("sess"),
            P(),
            P("sess", "mp"),
            P("sess", None, "mp", None),
            P("sess", None, None, "mp", None),
        ),
        out_specs=(P("sess", "mp"), P("sess", "mp", None, None), P("sess", "mp")),
        check_vma=False,
    )
```

time: 903 us -> 226 us (0.25)
  Pallas kernels: 675 us -> 76.6 us
  starting transfers between devices: 149 us -> 60.4 us
  waiting for transfers between devices: 0.94 us -> 61 us
  loops' own time: 38 us -> 0.66 us
    pallas_call x11, Pallas kernels: 633 us -> 32.8 us  [gather(): pl.pallas_call(functools.partial(gather_kernel, t), in_specs=[smem, smem]...]
    ppermute x44, starting transfers between devices: 133 us -> 50.1 us  [shift(): return lax.ppermute(block, 'sess', route)]
    ppermute x44, waiting for transfers between devices: 0.12 us -> 60.2 us  [shift(): return lax.ppermute(block, 'sess', route)]
    unnamed x1 -> x0, loops' own time: 38 us -> none
    pallas_call x2 -> x4, Pallas kernels: 30.2 us -> 32 us  [the longest x1 22.7 us: sessions(): pl.pallas_call(session_kernel, grid=(slots + 1,), in_specs=[smem, smem, s...]
  transfers between devices with their start and end apart: 45 -> 45, of which waited for: 1 -> 15; matrix products, arithmetic and copies ran while one was open for 1% -> 4% of each run, Pallas kernels for 63% -> 21%
where the time goes in v2:
time: 226 us; the launch traced here: 225 us
  Pallas kernels  76.6 us (34%)
  waiting for transfers between devices  61 us (27%)
  starting transfers between devices  60.4 us (27%)
  local copies, waits for them, and re-layouts  14.3 us (6%)
  other arithmetic  9.6 us (4%)
    ppermute x44, waiting for transfers between devices, shift(): return lax.ppermute(block, 'sess', route)  60.2 us
    ppermute x44, starting transfers between devices, shift(): return lax.ppermute(block, 'sess', route)  50.1 us
    pallas_call x11, Pallas kernels, gather(): pl.pallas_call(functools.partial(gather_kernel, t), in_specs=[smem, smem]...  32.8 us
    pallas_call x1, Pallas kernels, sessions(): pl.pallas_call(session_kernel, grid=(slots + 1,), in_specs=[smem, smem, s...  22.7 us
    pallas_call x1, Pallas kernels, mamba_before(): pl.pallas_call(before_kernel, grid=(slots,), in_specs=[per((tokens, width...  11.8 us
    ppermute x1, starting transfers between devices, swapped(): return lax.ppermute(block, axis, route)  10.3 us
    pallas_call x2, Pallas kernels, schedule(): pl.pallas_call(functools.partial(schedule_kernel, first, last), out_shape...  9.33 us
  transfers between devices with their start and end apart: 45, of which 15 were waited for; matrix products, arithmetic and copies ran while one was open for 4% of the time, Pallas kernels for 21%

profile of v2, /device:TPU:1, one launch (start us, length us, event | category | flops | bytes accessed | tf_op | source)
XLA Modules:
  0.0 224.5 jit_solution(10438324210474313856)
XLA Ops:
  5.7 4.4 %reshape.188.pool.previous = bf16[64,64,256]{2,1,0:T(8,128)(2,1)} reshape(bf16[64,64,2,1,128]{4,2,3,1,0:T(2,128)(2,1)} %param.43) | data formatting | bytes 4194304 | tf_op jit(solution)/shard_map/reshape | solution.py:490
  11.5 3.3 %gather_step.23 = (bf16[1280,256]{1,0:T(8,128)(2,1)}, bf16[1280,256]{1,0:T(8,128)(2,1)}, bf16[1280,256]{1,0:T(8,128)(2,1)}, bf16[1280,256]{1,0:T(8,128)(2,1)}) custom-call(s32[128]{0:T(128)} %fusion.4.codes, s32[64]{0:T(128)S(1)} %reshape.183.pages, bf16[16,1024,256]{2,1,0:T(8,128)(2,1)} %bitcast.58, bf16[64,64,256]{2,1,0:T(8,128)(2,1)} %reshape.188.pool.previous, ...), custom_call_target="tpu_custom_call" | custom-call | bytes 5242880 | tf_op jit(solution)/shard_map/gather_step/pallas_call | solution.py:312
  21.1 7.6 %schedule.3 = (s32[16,128]{1,0:T(8,128)}, s32[8,256]{1,0:T(8,128)S(1)}) custom-call(s32[1,256]{1,0:T(1,128)} %and_select_fusion.dest_ref, s32[16,128]{1,0:T(8,128)} %get-tuple-element.1909.refs_0_, s32[8,256]{1,0:T(8,128)} %get-tuple-element.1910.refs_1_), custom_call_target="tpu_custom_call" | custom-call | flops 10000000 | bytes 1048576 | tf_op jit(solution)/shard_map/schedule/pallas_call | solution.py:244
  29.4 3.2 %gather_step.24 = (bf16[1280,256]{1,0:T(8,128)(2,1)}, bf16[1280,256]{1,0:T(8,128)(2,1)}, bf16[1280,256]{1,0:T(8,128)(2,1)}, bf16[1280,256]{1,0:T(8,128)(2,1)}) custom-call(s32[128]{0:T(128)S(1)} %fusion.3.codes, s32[64]{0:T(128)S(1)} %reshape.183.pages, bf16[16,1024,256]{2,1,0:T(8,128)(2,1)} %bitcast.59, bf16[64,64,256]{2,1,0:T(8,128)(2,1)S(1)} %copy-done.2, ...), custom_call_target="tpu_custom_call" | custom-call | bytes 5242880 | tf_op jit(solution)/shard_map/gather_step/pallas_call | solution.py:312
  38.0 3.9 %gather_step.25 = (bf16[1280,256]{1,0:T(8,128)(2,1)}, bf16[1280,256]{1,0:T(8,128)(2,1)}, bf16[1280,256]{1,0:T(8,128)(2,1)}, bf16[1280,256]{1,0:T(8,128)(2,1)}) custom-call(s32[128]{0:T(128)S(1)} %fusion.3.codes, s32[64]{0:T(128)S(1)} %reshape.183.pages, bf16[16,1024,256]{2,1,0:T(8,128)(2,1)} %bitcast.60, bf16[64,64,256]{2,1,0:T(8,128)(2,1)S(1)} %copy-done.2, ...), custom_call_target="tpu_custom_call" | custom-call | bytes 5242880 | tf_op jit(solution)/shard_map/gather_step/pallas_call | solution.py:312
  42.0 6.8 %collective-permute-done.21.refs_4_ = bf16[1280,256]{1,0:T(8,128)(2,1)} collective-permute-done((bf16[1280,256]{1,0:T(8,128)(2,1)}, bf16[1280,256]{1,0:T(8,128)(2,1)}, u32[]{:S(2)}, u32[]{:S(2)}) %collective-permute-start.21) | collective-permute-done | bytes 655392 | tf_op jit(solution)/shard_map/ppermute | solution.py:352
  51.5 3.3 %gather_step.26 = (bf16[1280,256]{1,0:T(8,128)(2,1)}, bf16[1280,256]{1,0:T(8,128)(2,1)}, bf16[1280,256]{1,0:T(8,128)(2,1)}, bf16[1280,256]{1,0:T(8,128)(2,1)}) custom-call(s32[128]{0:T(128)S(1)} %fusion.3.codes, s32[64]{0:T(128)S(1)} %reshape.183.pages, bf16[16,1024,256]{2,1,0:T(8,128)(2,1)} %bitcast.61, bf16[64,64,256]{2,1,0:T(8,128)(2,1)S(1)} %copy-done.2, ...), custom_call_target="tpu_custom_call" | custom-call | bytes 5242880 | tf_op jit(solution)/shard_map/gather_step/pallas_call | solution.py:312
  56.3 6.5 %collective-permute-done.25.refs_8_ = bf16[1280,256]{1,0:T(8,128)(2,1)} collective-permute-done((bf16[1280,256]{1,0:T(8,128)(2,1)}, bf16[1280,256]{1,0:T(8,128)(2,1)}, u32[]{:S(2)}, u32[]{:S(2)}) %collective-permute-start.25) | collective-permute-done | bytes 655392 | tf_op jit(solution)/shard_map/ppermute | solution.py:352
  65.5 3.5 %gather_step.27 = (bf16[1280,256]{1,0:T(8,128)(2,1)}, bf16[1280,256]{1,0:T(8,128)(2,1)}, bf16[1280,256]{1,0:T(8,128)(2,1)}, bf16[1280,256]{1,0:T(8,128)(2,1)}) custom-call(s32[128]{0:T(128)S(1)} %fusion.3.codes, s32[64]{0:T(128)S(1)} %reshape.183.pages, bf16[16,1024,256]{2,1,0:T(8,128)(2,1)} %bitcast.62, bf16[64,64,256]{2,1,0:T(8,128)(2,1)S(1)} %copy-done.2, ...), custom_call_target="tpu_custom_call" | custom-call | bytes 5242880 | tf_op jit(solution)/shard_map/gather_step/pallas_call | solution.py:312
  70.8 6.1 %collective-permute-done.29.refs_12_ = bf16[1280,256]{1,0:T(8,128)(2,1)} collective-permute-done((bf16[1280,256]{1,0:T(8,128)(2,1)}, bf16[1280,256]{1,0:T(8,128)(2,1)}, u32[]{:S(2)}, u32[]{:S(2)}) %collective-permute-start.29) | collective-permute-done | bytes 655392 | tf_op jit(solution)/shard_map/ppermute | solution.py:352
  79.6 3.9 %gather_step.28 = (bf16[1280,256]{1,0:T(8,128)(2,1)}, bf16[1280,256]{1,0:T(8,128)(2,1)}, bf16[1280,256]{1,0:T(8,128)(2,1)}, bf16[1280,256]{1,0:T(8,128)(2,1)}) custom-call(s32[128]{0:T(128)S(1)} %fusion.3.codes, s32[64]{0:T(128)S(1)} %reshape.183.pages, bf16[16,1024,256]{2,1,0:T(8,128)(2,1)} %bitcast.63, bf16[64,64,256]{2,1,0:T(8,128)(2,1)S(1)} %copy-done.2, ...), custom_call_target="tpu_custom_call" | custom-call | bytes 5242880 | tf_op jit(solution)/shard_map/gather_step/pallas_call | solution.py:312
  84.8 6.1 %collective-permute-done.33.refs_16_ = bf16[1280,256]{1,0:T(8,128)(2,1)} collective-permute-done((bf16[1280,256]{1,0:T(8,128)(2,1)}, bf16[1280,256]{1,0:T(8,128)(2,1)}, u32[]{:S(2)}, u32[]{:S(2)}) %collective-permute-start.33) | collective-permute-done | bytes 655392 | tf_op jit(solution)/shard_map/ppermute | solution.py:352
  93.6 3.9 %gather_step.29 = (bf16[1280,256]{1,0:T(8,128)(2,1)}, bf16[1280,256]{1,0:T(8,128)(2,1)}, bf16[1280,256]{1,0:T(8,128)(2,1)}, bf16[1280,256]{1,0:T(8,128)(2,1)}) custom-call(s32[128]{0:T(128)S(1)} %fusion.3.codes, s32[64]{0:T(128)S(1)} %reshape.183.pages, bf16[16,1024,256]{2,1,0:T(8,128)(2,1)} %bitcast.64, bf16[64,64,256]{2,1,0:T(8,128)(2,1)S(1)} %copy-done.2, ...), custom_call_target="tpu_custom_call" | custom-call | bytes 5242880 | tf_op jit(solution)/shard_map/gather_step/pallas_call | solution.py:312
  98.4 6.5 %collective-permute-done.37.refs_20_ = bf16[1280,256]{1,0:T(8,128)(2,1)} collective-permute-done((bf16[1280,256]{1,0:T(8,128)(2,1)}, bf16[1280,256]{1,0:T(8,128)(2,1)}, u32[]{:S(2)}, u32[]{:S(2)}) %collective-permute-start.37) | collective-permute-done | bytes 655392 | tf_op jit(solution)/shard_map/ppermute | solution.py:352
  107.9 3.1 %gather_step.30 = (bf16[1280,256]{1,0:T(8,128)(2,1)}, bf16[1280,256]{1,0:T(8,128)(2,1)}, bf16[1280,256]{1,0:T(8,128)(2,1)}, bf16[1280,256]{1,0:T(8,128)(2,1)}) custom-call(s32[128]{0:T(128)S(1)} %fusion.3.codes, s32[64]{0:T(128)S(1)} %reshape.183.pages, bf16[16,1024,256]{2,1,0:T(8,128)(2,1)} %bitcast.65, bf16[64,64,256]{2,1,0:T(8,128)(2,1)S(1)} %copy-done.2, ...), custom_call_target="tpu_custom_call" | custom-call | bytes 5242880 | tf_op jit(solution)/shard_map/gather_step/pallas_call | solution.py:312
  112.1 6.9 %collective-permute-done.41.refs_24_ = bf16[1280,256]{1,0:T(8,128)(2,1)} collective-permute-done((bf16[1280,256]{1,0:T(8,128)(2,1)}, bf16[1280,256]{1,0:T(8,128)(2,1)}, u32[]{:S(2)}, u32[]{:S(2)}) %collective-permute-start.41) | collective-permute-done | bytes 655392 | tf_op jit(solution)/shard_map/ppermute | solution.py:352
  127.4 5.6 %collective-permute-done.45.refs_28_ = bf16[1280,256]{1,0:T(8,128)(2,1)} collective-permute-done((bf16[1280,256]{1,0:T(8,128)(2,1)}, bf16[1280,256]{1,0:T(8,128)(2,1)}, u32[]{:S(2)}, u32[]{:S(2)}) %collective-permute-start.45) | collective-permute-done | bytes 655392 | tf_op jit(solution)/shard_map/ppermute | solution.py:352
  141.8 3.3 %collective-permute-start.56 = (bf16[1280,256]{1,0:T(8,128)(2,1)}, bf16[1280,256]{1,0:T(8,128)(2,1)}, u32[]{:S(2)}, u32[]{:S(2)}) collective-permute-start(bf16[1280,256]{1,0:T(8,128)(2,1)} %get-tuple-element.1954), channel_id=1, source_target_pairs={{0,96},{8,104},{16,112},{24,120},{32,0},{40,8},{48,16},{56,24},{64... | collective-permute-start | bytes 1966088 | tf_op jit(solution)/shard_map/ppermute | solution.py:352
  154.3 11.8 %mamba_before.1 = (f32[512,1024]{1,0:T(8,128)}, bf16[512,1024]{1,0:T(8,128)(2,1)}) custom-call(bf16[512,1024]{1,0:T(8,128)(2,1)} %x_ref.1, bf16[512,256]{1,0:T(8,128)(2,1)} %get-tuple-element.2121.b_ref.b, bf16[512,256]{1,0:T(8,128)(2,1)} %get-tuple-element.2120.c_ref.c, f32[16,32,16]{2,1,0:T(8,128)} %bitcast.70, ...), custom_call_target="tpu_custom_call" | custom-call | flops 1000000000 | bytes 20971520 | tf_op jit(solution)/shard_map/mamba_before/pallas_call | solution.py:97
  167.6 17.5 %conditional.4 = ((bf16[1280,256]{1,0:T(8,128)(2,1)}, bf16[1280,256]{1,0:T(8,128)(2,1)}, bf16[1280,256]{1,0:T(8,128)(2,1)}, bf16[1280,256]{1,0:T(8,128)(2,1)}, b...) conditional(s32[]{:T(128)} %convert_element_type.29, () %tuple.86, ...), branch_computations={%region_4.5_spmd, %region_5.18_spmd} | conditional | flops 330293 | bytes 76691272 | solution.py:540
  172.8 3.7 %collective-permute-start.16 = (bf16[1280,256]{1,0:T(8,128)(2,1)}, bf16[1280,256]{1,0:T(8,128)(2,1)}, u32[]{:S(2)}, u32[]{:S(2)}) collective-permute-start(bf16[1280,256]{1,0:T(8,128)(2,1)} %get-tuple-element.1816), channel_id=1, source_target_pairs={{0,96},{8,104},{16,112},{24,120},{32,0},{40,8},{48,16},{56,24},{64... | collective-permute-start | bytes 1966088 | tf_op jit(solution)/shard_map/cond/branch_1_fun/ppermute | solution.py:352
  179.6 5.5 %collective-permute-done.15 = bf16[1280,256]{1,0:T(8,128)(2,1)} collective-permute-done((bf16[1280,256]{1,0:T(8,128)(2,1)}, bf16[1280,256]{1,0:T(8,128)(2,1)}, u32[]{:S(2)}, u32[]{:S(2)}) %collective-permute-start.15) | collective-permute-done | bytes 655392 | tf_op jit(solution)/shard_map/cond/branch_1_fun/ppermute | solution.py:352
  185.9 22.7 %sessions.1 = (f32[512,1024]{1,0:T(8,128)}, f32[16,1,32]{2,1,0:T(1,128)}, bf16[16,16,64,256]{3,2,1,0:T(8,128)(2,1)}, bf16[512,1024]{1,0:T(8,128)(2,1)}) custom-call(s32[16]{0:T(128)} %select_reduce_fusion.1.codes, s32[64]{0:T(128)S(1)} %reshape.183.pages, s32[16]{0:T(128)} %prefix.1, f32[512,1024]{1,0:T(8,128)} %get-tuple-element.1912.base, ...), custom_call_target="tpu_custom_call" | custom-call | flops 2000000000 | bytes 33554432 | tf_op jit(solution)/shard_map/sessions/pallas_call | solution.py:405
  210.5 10.3 %collective-permute-start.57 = (f32[512]{0:T(512)S(1)}, f32[512]{0:T(512)S(1)}, u32[]{:S(2)}, u32[]{:S(2)}) collective-permute-start(f32[512]{0:T(512)S(1)} %reshape.189), channel_id=1, source_target_pairs={{0,1},{1,0},{2,3},{3,2},{4,5},{5,4},{6,7},{7,6},{8,9},{9,8},{10,11... | collective-permute-start | bytes 6152 | tf_op jit(solution)/shard_map/ppermute | solution.py:43
  (149 shorter events, 80.2 us)
Async XLA Ops:
  14.8 17.9 %collective-permute-start.17 = (bf16[1280,256]{1,0:T(8,128)(2,1)}, bf16[1280,256]{1,0:T(8,128)(2,1)}, u32[]{:S(2)}, u32[]{:S(2)}) collective-permute-start(bf16[1280,256]{1,0:T(8,128)(2,1)} %get-tuple-element.1914.previous), channel_id=1, source_target_pairs={{0,8},{8,16},{16,24},{24,0},{32,40},{40,48},{48,56},{56,32},{64,72... | collective-permute-start | bytes 1966088 | tf_op jit(solution)/shard_map/ppermute | solution.py:352
  16.9 18.4 %collective-permute-start.18 = (bf16[1280,256]{1,0:T(8,128)(2,1)}, bf16[1280,256]{1,0:T(8,128)(2,1)}, u32[]{:S(2)}, u32[]{:S(2)}) collective-permute-start(bf16[1280,256]{1,0:T(8,128)(2,1)} %get-tuple-element.1915), channel_id=1, source_target_pairs={{0,24},{8,0},{16,8},{24,16},{32,56},{40,32},{48,40},{56,48},{64,88... | collective-permute-start | bytes 1966088 | tf_op jit(solution)/shard_map/ppermute | solution.py:352
  18.3 17.1 %collective-permute-start.19 = (bf16[1280,256]{1,0:T(8,128)(2,1)}, bf16[1280,256]{1,0:T(8,128)(2,1)}, u32[]{:S(2)}, u32[]{:S(2)}) collective-permute-start(bf16[1280,256]{1,0:T(8,128)(2,1)} %get-tuple-element.1916), channel_id=1, source_target_pairs={{0,32},{8,40},{16,48},{24,56},{32,64},{40,72},{48,80},{56,88},{64,... | collective-permute-start | bytes 1966088 | tf_op jit(solution)/shard_map/ppermute | solution.py:352
  19.7 18.4 %collective-permute-start.20 = (bf16[1280,256]{1,0:T(8,128)(2,1)}, bf16[1280,256]{1,0:T(8,128)(2,1)}, u32[]{:S(2)}, u32[]{:S(2)}) collective-permute-start(bf16[1280,256]{1,0:T(8,128)(2,1)} %get-tuple-element.1917), channel_id=1, source_target_pairs={{0,96},{8,104},{16,112},{24,120},{32,0},{40,8},{48,16},{56,24},{64... | collective-permute-start | bytes 1966088 | tf_op jit(solution)/shard_map/ppermute | solution.py:352
  32.6 16.2 %collective-permute-start.21 = (bf16[1280,256]{1,0:T(8,128)(2,1)}, bf16[1280,256]{1,0:T(8,128)(2,1)}, u32[]{:S(2)}, u32[]{:S(2)}) collective-permute-start(bf16[1280,256]{1,0:T(8,128)(2,1)} %get-tuple-element.1919.previous), channel_id=1, source_target_pairs={{0,8},{8,16},{16,24},{24,0},{32,40},{40,48},{48,56},{56,32},{64,72... | collective-permute-start | bytes 1966088 | tf_op jit(solution)/shard_map/ppermute | solution.py:352
  32.7 16.1 %collective-permute-start.22 = (bf16[1280,256]{1,0:T(8,128)(2,1)}, bf16[1280,256]{1,0:T(8,128)(2,1)}, u32[]{:S(2)}, u32[]{:S(2)}) collective-permute-start(bf16[1280,256]{1,0:T(8,128)(2,1)} %get-tuple-element.1920), channel_id=1, source_target_pairs={{0,24},{8,0},{16,8},{24,16},{32,56},{40,32},{48,40},{56,48},{64,88... | collective-permute-start | bytes 1966088 | tf_op jit(solution)/shard_map/ppermute | solution.py:352
  35.4 15.5 %collective-permute-start.23 = (bf16[1280,256]{1,0:T(8,128)(2,1)}, bf16[1280,256]{1,0:T(8,128)(2,1)}, u32[]{:S(2)}, u32[]{:S(2)}) collective-permute-start(bf16[1280,256]{1,0:T(8,128)(2,1)} %get-tuple-element.1921), channel_id=1, source_target_pairs={{0,32},{8,40},{16,48},{24,56},{32,64},{40,72},{48,80},{56,88},{64,... | collective-permute-start | bytes 1966088 | tf_op jit(solution)/shard_map/ppermute | solution.py:352
  35.4 16.1 %collective-permute-start.24 = (bf16[1280,256]{1,0:T(8,128)(2,1)}, bf16[1280,256]{1,0:T(8,128)(2,1)}, u32[]{:S(2)}, u32[]{:S(2)}) collective-permute-start(bf16[1280,256]{1,0:T(8,128)(2,1)} %get-tuple-element.1922), channel_id=1, source_target_pairs={{0,96},{8,104},{16,112},{24,120},{32,0},{40,8},{48,16},{56,24},{64... | collective-permute-start | bytes 1966088 | tf_op jit(solution)/shard_map/ppermute | solution.py:352
  41.9 20.9 %collective-permute-start.25 = (bf16[1280,256]{1,0:T(8,128)(2,1)}, bf16[1280,256]{1,0:T(8,128)(2,1)}, u32[]{:S(2)}, u32[]{:S(2)}) collective-permute-start(bf16[1280,256]{1,0:T(8,128)(2,1)} %get-tuple-element.1923.previous), channel_id=1, source_target_pairs={{0,8},{8,16},{16,24},{24,0},{32,40},{40,48},{48,56},{56,32},{64,72... | collective-permute-start | bytes 1966088 | tf_op jit(solution)/shard_map/ppermute | solution.py:352
  54.8 22.1 %collective-permute-start.29 = (bf16[1280,256]{1,0:T(8,128)(2,1)}, bf16[1280,256]{1,0:T(8,128)(2,1)}, u32[]{:S(2)}, u32[]{:S(2)}) collective-permute-start(bf16[1280,256]{1,0:T(8,128)(2,1)} %get-tuple-element.1927.previous), channel_id=1, source_target_pairs={{0,8},{8,16},{16,24},{24,0},{32,40},{40,48},{48,56},{56,32},{64,72... | collective-permute-start | bytes 1966088 | tf_op jit(solution)/shard_map/ppermute | solution.py:352
  62.9 16.7 %collective-permute-start.32 = (bf16[1280,256]{1,0:T(8,128)(2,1)}, bf16[1280,256]{1,0:T(8,128)(2,1)}, u32[]{:S(2)}, u32[]{:S(2)}) collective-permute-start(bf16[1280,256]{1,0:T(8,128)(2,1)} %get-tuple-element.1930), channel_id=1, source_target_pairs={{0,96},{8,104},{16,112},{24,120},{32,0},{40,8},{48,16},{56,24},{64... | collective-permute-start | bytes 1966088 | tf_op jit(solution)/shard_map/ppermute | solution.py:352
  69.1 21.9 %collective-permute-start.33 = (bf16[1280,256]{1,0:T(8,128)(2,1)}, bf16[1280,256]{1,0:T(8,128)(2,1)}, u32[]{:S(2)}, u32[]{:S(2)}) collective-permute-start(bf16[1280,256]{1,0:T(8,128)(2,1)} %get-tuple-element.1931.previous), channel_id=1, source_target_pairs={{0,8},{8,16},{16,24},{24,0},{32,40},{40,48},{48,56},{56,32},{64,72... | collective-permute-start | bytes 1966088 | tf_op jit(solution)/shard_map/ppermute | solution.py:352
  76.9 16.7 %collective-permute-start.36 = (bf16[1280,256]{1,0:T(8,128)(2,1)}, bf16[1280,256]{1,0:T(8,128)(2,1)}, u32[]{:S(2)}, u32[]{:S(2)}) collective-permute-start(bf16[1280,256]{1,0:T(8,128)(2,1)} %get-tuple-element.1934), channel_id=1, source_target_pairs={{0,96},{8,104},{16,112},{24,120},{32,0},{40,8},{48,16},{56,24},{64... | collective-permute-start | bytes 1966088 | tf_op jit(solution)/shard_map/ppermute | solution.py:352
  83.5 21.5 %collective-permute-start.37 = (bf16[1280,256]{1,0:T(8,128)(2,1)}, bf16[1280,256]{1,0:T(8,128)(2,1)}, u32[]{:S(2)}, u32[]{:S(2)}) collective-permute-start(bf16[1280,256]{1,0:T(8,128)(2,1)} %get-tuple-element.1935.previous), channel_id=1, source_target_pairs={{0,8},{8,16},{16,24},{24,0},{32,40},{40,48},{48,56},{56,32},{64,72... | collective-permute-start | bytes 1966088 | tf_op jit(solution)/shard_map/ppermute | solution.py:352
  91.0 16.9 %collective-permute-start.40 = (bf16[1280,256]{1,0:T(8,128)(2,1)}, bf16[1280,256]{1,0:T(8,128)(2,1)}, u32[]{:S(2)}, u32[]{:S(2)}) collective-permute-start(bf16[1280,256]{1,0:T(8,128)(2,1)} %get-tuple-element.1938), channel_id=1, source_target_pairs={{0,96},{8,104},{16,112},{24,120},{32,0},{40,8},{48,16},{56,24},{64... | collective-permute-start | bytes 1966088 | tf_op jit(solution)/shard_map/ppermute | solution.py:352
  97.5 21.5 %collective-permute-start.41 = (bf16[1280,256]{1,0:T(8,128)(2,1)}, bf16[1280,256]{1,0:T(8,128)(2,1)}, u32[]{:S(2)}, u32[]{:S(2)}) collective-permute-start(bf16[1280,256]{1,0:T(8,128)(2,1)} %get-tuple-element.1939.previous), channel_id=1, source_target_pairs={{0,8},{8,16},{16,24},{24,0},{32,40},{40,48},{48,56},{56,32},{64,72... | collective-permute-start | bytes 1966088 | tf_op jit(solution)/shard_map/ppermute | solution.py:352
  105.2 19.5 %collective-permute-start.44 = (bf16[1280,256]{1,0:T(8,128)(2,1)}, bf16[1280,256]{1,0:T(8,128)(2,1)}, u32[]{:S(2)}, u32[]{:S(2)}) collective-permute-start(bf16[1280,256]{1,0:T(8,128)(2,1)} %get-tuple-element.1942), channel_id=1, source_target_pairs={{0,96},{8,104},{16,112},{24,120},{32,0},{40,8},{48,16},{56,24},{64... | collective-permute-start | bytes 1966088 | tf_op jit(solution)/shard_map/ppermute | solution.py:352
  111.0 22.0 %collective-permute-start.45 = (bf16[1280,256]{1,0:T(8,128)(2,1)}, bf16[1280,256]{1,0:T(8,128)(2,1)}, u32[]{:S(2)}, u32[]{:S(2)}) collective-permute-start(bf16[1280,256]{1,0:T(8,128)(2,1)} %get-tuple-element.1943.previous), channel_id=1, source_target_pairs={{0,8},{8,16},{16,24},{24,0},{32,40},{40,48},{48,56},{56,32},{64,72... | collective-permute-start | bytes 1966088 | tf_op jit(solution)/shard_map/ppermute | solution.py:352
  119.0 15.0 %collective-permute-start.48 = (bf16[1280,256]{1,0:T(8,128)(2,1)}, bf16[1280,256]{1,0:T(8,128)(2,1)}, u32[]{:S(2)}, u32[]{:S(2)}) collective-permute-start(bf16[1280,256]{1,0:T(8,128)(2,1)} %get-tuple-element.1946), channel_id=1, source_target_pairs={{0,96},{8,104},{16,112},{24,120},{32,0},{40,8},{48,16},{56,24},{64... | collective-permute-start | bytes 1966088 | tf_op jit(solution)/shard_map/ppermute | solution.py:352
  141.8 25.1 %collective-permute-start.49 = (bf16[1280,256]{1,0:T(8,128)(2,1)}, bf16[1280,256]{1,0:T(8,128)(2,1)}, u32[]{:S(2)}, u32[]{:S(2)}) collective-permute-start(bf16[1280,256]{1,0:T(8,128)(2,1)} %get-tuple-element.1947.previous), channel_id=1, source_target_pairs={{0,8},{8,16},{16,24},{24,0},{32,40},{40,48},{48,56},{56,32},{64,72... | collective-permute-start | bytes 1966088 | tf_op jit(solution)/shard_map/ppermute | solution.py:352
  141.8 25.1 %collective-permute-start.56 = (bf16[1280,256]{1,0:T(8,128)(2,1)}, bf16[1280,256]{1,0:T(8,128)(2,1)}, u32[]{:S(2)}, u32[]{:S(2)}) collective-permute-start(bf16[1280,256]{1,0:T(8,128)(2,1)} %get-tuple-element.1954), channel_id=1, source_target_pairs={{0,96},{8,104},{16,112},{24,120},{32,0},{40,8},{48,16},{56,24},{64... | collective-permute-start | bytes 1966088 | tf_op jit(solution)/shard_map/ppermute | solution.py:352
  148.2 18.7 %collective-permute-start.50 = (bf16[1280,256]{1,0:T(8,128)(2,1)}, bf16[1280,256]{1,0:T(8,128)(2,1)}, u32[]{:S(2)}, u32[]{:S(2)}) collective-permute-start(bf16[1280,256]{1,0:T(8,128)(2,1)} %get-tuple-element.1948), channel_id=1, source_target_pairs={{0,24},{8,0},{16,8},{24,16},{32,56},{40,32},{48,40},{56,48},{64,88... | collective-permute-start | bytes 1966088 | tf_op jit(solution)/shard_map/ppermute | solution.py:352
  149.1 17.8 %collective-permute-start.51 = (bf16[1280,256]{1,0:T(8,128)(2,1)}, bf16[1280,256]{1,0:T(8,128)(2,1)}, u32[]{:S(2)}, u32[]{:S(2)}) collective-permute-start(bf16[1280,256]{1,0:T(8,128)(2,1)} %get-tuple-element.1949), channel_id=1, source_target_pairs={{0,32},{8,40},{16,48},{24,56},{32,64},{40,72},{48,80},{56,88},{64,... | collective-permute-start | bytes 1966088 | tf_op jit(solution)/shard_map/ppermute | solution.py:352
  150.2 17.4 %collective-permute-start.52 = (bf16[1280,256]{1,0:T(8,128)(2,1)}, bf16[1280,256]{1,0:T(8,128)(2,1)}, u32[]{:S(2)}, u32[]{:S(2)}) collective-permute-start(bf16[1280,256]{1,0:T(8,128)(2,1)} %get-tuple-element.1950), channel_id=1, source_target_pairs={{0,96},{8,104},{16,112},{24,120},{32,0},{40,8},{48,16},{56,24},{64... | collective-permute-start | bytes 1966088 | tf_op jit(solution)/shard_map/ppermute | solution.py:352
  (32 other events, 580.7 us)
